TPU v7x, 256 devices: a whole 4x4x8 slice. The times are simulated.
256 devices in a mesh: dp: 16 (over z, core), seq: 16 (over y, x).
Axes of the slice: x: 4, y: 4, z: 8, core: 2. Of those that a mesh axis runs over, the one named last changes fastest.
Arguments:
- queries: bfloat16 [16, 4096, 2240], P('dp', 'seq'), may hold values from -6 to 6
- keys: bfloat16 [16, 4096, 2240], P('dp', 'seq'), may hold values from -1.5 to 1.5
- values: bfloat16 [16, 4096, 2240], P('dp', 'seq'), may hold values from -7 to 7
- cotangent: bfloat16 [16, 4096, 2240], P('dp', 'seq'), may hold values from -6 to 6
- conv_weight: float32 [2, 2240], replicated, may hold values from -3 to 3
Outputs:
- mixed: bfloat16 [16, 4096, 2240], P('dp', 'seq')
- grad_queries: bfloat16 [16, 4096, 2240], P('dp', 'seq')
- grad_keys: bfloat16 [16, 4096, 2240], P('dp', 'seq')
- grad_values: bfloat16 [16, 4096, 2240], P('dp', 'seq')
- conv_grad: float32 [2, 2240], replicated
All inputs are finite; a program needn't handle non-finite values.
Results may differ from a plain program's by a relative error of at most 0.0047.
Values may be sent and summed in bfloat16 or wider, within the bound.
No kernel may reach another device: no remote copies, remote signals or barrier semaphores. Data moves between devices by JAX's collectives and lax.ppermute only.
A program may use at most 128 MiB of HBM per device.

v0:
```python
import jax
import jax.numpy as jnp
from jax import lax
from jax.sharding import PartitionSpec as P

HEADS = 20
HEAD_DIM = 112
FRAME = 128


denom_eps = 1e-06
loss_scale = 16.0


def entering(value, axis, join, neutral, backward):
    count, mine = (lax.axis_size(axis), lax.axis_index(axis))
    pieces = jax.tree.map(lambda part: lax.all_gather(part, axis), value)
    if backward:
        pieces = jax.tree.map(lambda part: part[::-1], pieces)
        mine = count - 1 - mine
    subtotal = jax.tree.map(
        lambda part, zero: jnp.full_like(part, 0) + jnp.asarray(zero, part.dtype), value, neutral
    )

    def step(position, subtotal):
        longer = join(subtotal, jax.tree.map(lambda part: part[position], pieces))
        return jax.tree.map(lambda new, old: jnp.where(position < mine, new, old), longer, subtotal)

    return lax.fori_loop(0, count - 1, step, subtotal)


def from_behind(block, axis, distance):
    devices = range(lax.axis_size(axis))
    route = [(i - distance, i) for i in devices if i - distance in devices]
    return lax.ppermute(block, axis, route)


def add_pair(first_part, second_part):
    return (first_part[0] + second_part[0], first_part[1] + second_part[1])


def suffix_sum(blocks):
    return jnp.flip(jnp.cumsum(jnp.flip(blocks, 1), 1), 1)


def body(queries, keys, values, cotangent, conv_weight):
    mixed_prec = lax.Precision.HIGH
    f32 = jnp.float32
    clip_count, tok_rows, feature_width = queries.shape
    frame_count = tok_rows // FRAME
    frame_shape = (clip_count, frame_count, FRAME, HEADS, HEAD_DIM)
    q_feat = jnp.maximum(queries, 0).reshape(frame_shape)
    k_feat = jnp.maximum(keys, 0).reshape(frame_shape)
    v_frames = values.reshape(frame_shape)
    frame_kv = jnp.einsum("cfthe,cfthd->cfhed", k_feat, v_frames, preferred_element_type=f32)
    frame_keys = jnp.sum(k_feat, axis=2, dtype=f32)
    own_kv = jnp.sum(frame_kv, axis=1)
    own_keys = jnp.sum(frame_keys, axis=1)
    empty = (jnp.zeros_like(own_kv), jnp.zeros_like(own_keys))
    kv_prev, keys_prev = entering((own_kv, own_keys), "seq", add_pair, empty, False)
    kv_incl = kv_prev[:, None] + jnp.cumsum(frame_kv, axis=1)
    keys_incl = keys_prev[:, None] + jnp.cumsum(frame_keys, axis=1)
    denominator = (
        jnp.einsum(
            "cfthe,cfhe->cfth", q_feat, keys_incl, precision=mixed_prec, preferred_element_type=f32
        )
        + denom_eps
    )
    numerator = jnp.einsum(
        "cfthe,cfhed->cfthd", q_feat, kv_incl, precision=mixed_prec, preferred_element_type=f32
    )
    attended = (
        (numerator / denominator[..., None])
        .astype(jnp.bfloat16)
        .reshape(clip_count, tok_rows, feature_width)
    )
    prev_rim = from_behind(attended, "seq", 1)
    extended = jnp.concatenate([prev_rim, attended], axis=1)
    one_back = extended[:, FRAME : FRAME + tok_rows].astype(f32)
    two_back = extended[:, :tok_rows].astype(f32)
    mixed = (attended.astype(f32) + conv_weight[0] * one_back + conv_weight[1] * two_back).astype(
        jnp.bfloat16
    )
    next_head = from_behind(cotangent, "seq", -1)
    cot_ext = jnp.concatenate([cotangent, next_head], axis=1).astype(f32)
    cot_wide = cot_ext[:, :tok_rows]
    grad_out = loss_scale * (
        cot_wide
        + conv_weight[0] * cot_ext[:, FRAME : FRAME + tok_rows]
        + conv_weight[1] * cot_ext[:, 2 * FRAME : 2 * FRAME + tok_rows]
    )
    local_conv = jnp.stack(
        [jnp.sum(one_back * cot_wide, axis=(0, 1)), jnp.sum(two_back * cot_wide, axis=(0, 1))]
    )
    conv_grad = lax.psum(local_conv, ("dp", "seq")) / (clip_count * lax.axis_size("dp"))
    grad_frames = grad_out.reshape(frame_shape)
    grad_num = grad_frames / denominator[..., None]
    grad_den = -jnp.sum(grad_frames * numerator, -1) / (denominator * denominator)
    frame_grad = jnp.einsum(
        "cfthe,cfthd->cfhed", q_feat, grad_num, precision=mixed_prec, preferred_element_type=f32
    )
    frame_gkeys = jnp.einsum(
        "cfth,cfthe->cfhe", grad_den, q_feat, precision=mixed_prec, preferred_element_type=f32
    )
    own_grad = jnp.sum(frame_grad, axis=1)
    own_gkeys = jnp.sum(frame_gkeys, axis=1)
    blank = (jnp.zeros_like(own_grad), jnp.zeros_like(own_gkeys))
    grad_next, gkeys_next = entering((own_grad, own_gkeys), "seq", add_pair, blank, True)
    grad_incl = grad_next[:, None] + suffix_sum(frame_grad)
    gkeys_incl = gkeys_next[:, None] + suffix_sum(frame_gkeys)
    grad_q = (
        jnp.einsum(
            "cfthd,cfhed->cfthe",
            grad_num,
            kv_incl,
            precision=mixed_prec,
            preferred_element_type=f32,
        )
        + grad_den[..., None] * keys_incl[:, :, None]
    )
    grad_v = jnp.einsum(
        "cfthe,cfhed->cfthd", k_feat, grad_incl, precision=mixed_prec, preferred_element_type=f32
    )
    grad_k = (
        jnp.einsum(
            "cfthd,cfhed->cfthe",
            v_frames,
            grad_incl,
            precision=mixed_prec,
            preferred_element_type=f32,
        )
        + gkeys_incl[:, :, None]
    )
    out_shape = (clip_count, tok_rows, feature_width)
    grad_queries = jnp.where(queries > 0, grad_q.reshape(out_shape), 0.0).astype(jnp.bfloat16)
    grad_keys = jnp.where(keys > 0, grad_k.reshape(out_shape), 0.0).astype(jnp.bfloat16)
    grad_values = grad_v.reshape(out_shape).astype(jnp.bfloat16)
    return (mixed, grad_queries, grad_keys, grad_values, conv_grad)


def solution(mesh):
    return jax.shard_map(
        body,
        mesh=mesh,
        in_specs=(
            P("dp", "seq", None),
            P("dp", "seq", None),
            P("dp", "seq", None),
            P("dp", "seq", None),
            P(),
        ),
        out_specs=(
            P("dp", "seq", None),
            P("dp", "seq", None),
            P("dp", "seq", None),
            P("dp", "seq", None),
            P(),
        ),
        check_vma=False,
    )
```

profile of v0, /device:TPU:2, one launch (start us, length us, event | category | flops | bytes accessed | tf_op | source)
XLA Modules:
  0.0 470.5 jit_solution(8852168894574820605)
XLA Ops:
  7.2 2.8 reshape.217
  10.0 17.8 %fusion.47 = bf16[256,2240]{0,1:T(8,128)(2,1)} fusion(bf16[1,256,2240]{1,2,0:T(8,128)(2,1)S(1)} %copy-done.8), kind=kLoop, calls=%fused_computation.65 | loop fusion | flops 573440 | bytes 2293760 | tf_op jit(solution)/shard_map/max | solution.py:53
  27.8 2.7 reshape.216
  30.6 3.2 fusion.55
  33.9 4.4 collective-permute-start.1
  38.3 16.8 %convert_reduce_fusion.1 = f32[2240]{0:T(1024)S(1)} fusion(bf16[1,256,2240]{1,2,0:T(8,128)(2,1)S(1)} %copy-done.8), kind=kLoop, calls=%fused_computation.42 | loop fusion | flops 1718080 | bytes 1155840 | tf_op jit(solution)/shard_map/reduce_sum | solution.py:58
  55.2 18.7 %maximum_reduce_fusion = bf16[256,2240]{0,1:T(8,128)(2,1)} fusion(bf16[1,256,2240]{1,2,0:T(8,128)(2,1)} %param.9), kind=kLoop, calls=%fused_computation.41 | loop fusion | flops 573440 | bytes 2293760 | tf_op jit(solution)/shard_map/max | solution.py:52
  73.9 2.7 reshape.218
  76.7 3.5 convert_reduce_fusion
  80.2 10.2 %reduce_window_sum.37 = f32[2,20,112]{0,2,1:T(8,128)S(1)} reduce-window(f32[2,20,112]{0,2,1:T(8,128)} %convert_reduce_fusion, f32[]{:T(128)} %constant.68.clone.1), window={size=2x1x1 pad=1_0x0_0x0_0}, to_apply=%region_6.7 | reduce-window | flops 4480 | bytes 35844 | tf_op jit(solution)/shard_map/jit(cumsum)/reduce_window_sum | solution.py:62
  90.4 26.0 %all_gather.27 = f32[16,1,20,112]{3,1,2,0:T(1,128)} all-gather(f32[1,1,20,112]{3,1,2,0:T(1,128)S(1)} %all_gather.32), channel_id=1, replica_groups=mesh['dp'=16,'seq'=16] {'seq'}, dimensions={0}, use_global_device_ids=true | all-gather | bytes 152320 | tf_op jit(solution)/shard_map/all_gather | solution.py:17
  116.4 3.3 fusion.57
  119.6 55.9 %all-gather.7.cloned.1.call-done = f32[320,112,112]{2,1,0:T(8,128)} async-done(((f32[20,112,112]{2,1,0:T(8,128)}), f32[320,112,112]{2,1,0:T(8,128)}) %all-gather.7.cloned.1.call-update) | async-done | bytes 16056336 | tf_op jit(solution)/shard_map/all_gather | solution.py:17
  175.5 35.0 %while.32 = (s32[]{:T(128)}, f32[1,20,112,112]{3,2,1,0:T(8,128)S(1)}, f32[1,20,112]{2,1,0:T(8,128)S(1)}, s32[]{:T(128)}, f32[16,1,20,112,112]{4,3,2,1,0:T(8,128)...) while((s32[]{:T(128)}, f32[1,20,112,112]{3,2,1,0:T(8,128)S(1)}, ...), condition=%wide.region_3.4_spmd.clone, body=%wide.region_2.0_spmd.clone.sunk | while | flops 759364 | bytes 3055483 | solution.py:29
  176.2 1.6 add_select_fusion.8
  178.6 1.6 add_select_fusion.8
  180.9 1.6 add_select_fusion.8
  183.2 1.6 add_select_fusion.8
  185.6 1.6 add_select_fusion.8
  187.9 1.6 add_select_fusion.8
  190.2 1.6 add_select_fusion.8
  192.6 1.6 add_select_fusion.8
  194.9 1.6 add_select_fusion.8
  197.2 1.6 add_select_fusion.8
  199.6 1.6 add_select_fusion.8
  201.9 1.6 add_select_fusion.8
  211.9 1.6 copy.86
  214.2 4.4 fusion.17
  220.6 3.4 collective-permute-start
  224.1 2.2 maximum_convert_fusion
  226.4 23.2 %collective-permute-done = bf16[1,256,2240]{1,2,0:T(8,128)(2,1)S(1)} collective-permute-done((bf16[1,256,2240]{1,2,0:T(8,128)(2,1)S(1)}, bf16[1,256,2240]{1,2,0:T(8,128)(2,1)S(1)}, u32[]{:S(2)}, u32[]{:S(2)}) %collective-permute-start) | collective-permute-done | bytes 1146912 | tf_op jit(solution)/shard_map/ppermute | solution.py:35
  249.5 4.7 %fusion.3 = (f32[2240]{0:T(1024)S(1)}, f32[2240]{0:T(1024)S(1)}, f32[1,256,2240]{1,2,0:T(8,128)S(1)}, bf16[1,256,2240]{1,2,0:T(8,128)(2,1)}) fusion(f32[1,512,2240]{1,2,0:T(8,128)S(1)} %maximum_convert_fusion, bf16[1,256,2240]{1,2,0:T(8,128)(2,1)} %copy-done.10, bf16[1,256,2240]{1,2,0:T(8,128)(2,1)S(1)} %collective-permute-done, ...), kind=kLoop, calls=%fused_computation.15 | loop fusion | flops 11464320 | bytes 12651520 | tf_op jit(solution)/shard_map/reduce_sum | solution.py:93
  254.3 2.2 reshape.220
  256.4 6.3 %fusion.56 = (f32[20,112,112]{2,1,0:T(8,128)}, f32[2,20,112,112]{3,2,1,0:T(8,128)}) fusion(f32[2,128,20,112]{1,0,3,2:T(2,128)} %reshape.220, f32[2,128,20]{1,2,0:T(8,128)S(1)} %fusion.50, bf16[2,128,20,112]{1,0,3,2:T(2,128)(2,1)} %copy-done.6), kind=kOutput, calls=%fused_computation.85 | convolution fusion | flops 386176000 | bytes 6471680 | tf_op jit(solution)/shard_map/cfthe,cfthd->cfhed/dot_general | solution.py:99
  262.8 1.6 broadcast_add_fusion
  265.4 3.7 reshape.221
  269.2 2.8 fusion.18
  272.9 1.7 bitcast_add_fusion
  274.6 1.8 copy.73
  276.4 14.1 %fusion.5 = bf16[1,256,2240]{1,0,2:T(2,128)(2,1)S(1)} fusion(f32[1,256,2240]{1,0,2:T(1,128)S(1)} %bitcast.137, bf16[1,256,2240]{1,2,0:T(8,128)(2,1)S(1)} %copy-done.11), kind=kLoop, calls=%fused_computation.17 | loop fusion | flops 2293760 | bytes 4587520 | tf_op jit(solution)/shard_map/convert_element_type | solution.py:135
  293.4 3.3 reverse.6
  296.7 79.0 %psum.7 = f32[2,2240]{1,0:T(2,128)S(1)} all-reduce(f32[2,2240]{1,0:T(2,128)S(1)} %pad_maximum_fusion.1), channel_id=1, replica_groups=mesh['dp'=16,'seq'=16] {'dp','seq'}, use_global_device_ids=true, to_apply=%region_16.17 | all-reduce | flops 4480 | bytes 35840 | tf_op jit(solution)/shard_map/psum | solution.py:95
  375.7 22.5 %all-gather.3 = f32[16,20,112]{2,1,0:T(8,128)S(1)} all-gather(f32[1,20,112]{2,1,0:T(8,128)S(1)} %bitcast.144), channel_id=4, replica_groups=mesh['dp'=16,'seq'=16] {'seq'}, dimensions={0}, use_global_device_ids=true | all-gather | bytes 152320 | tf_op jit(solution)/shard_map/all_gather | solution.py:17
  398.3 3.2 fusion.15
  402.2 12.4 %rev.20 = f32[16,1,20,112,112]{4,3,2,1,0:T(8,128)} reverse(f32[16,1,20,112,112]{4,3,2,1,0:T(8,128)} %bitcast.136), dimensions={0} | reverse | bytes 32112640 | tf_op jit(solution)/shard_map/rev | solution.py:19
  414.6 24.6 %while.33 = (s32[]{:T(128)}, f32[1,20,112,112]{3,2,1,0:T(8,128)S(1)}, f32[1,20,112]{2,1,0:T(8,128)S(1)}, s32[]{:T(128)}, f32[16,1,20,112,112]{4,3,2,1,0:T(8,128)...) while((s32[]{:T(128)}, f32[1,20,112,112]{3,2,1,0:T(8,128)S(1)}, ...), condition=%wide.region_11.12_spmd.clone, body=%wide.region_10.11_spmd.clone.sunk | while | flops 759364 | bytes 3037563 | solution.py:29
  414.6 1.6 add_select_fusion.10
  416.2 1.6 add_select_fusion.10
  417.9 1.6 add_select_fusion.10
  419.5 1.6 add_select_fusion.10
  421.2 1.6 add_select_fusion.10
  422.8 1.6 add_select_fusion.10
  424.4 1.6 add_select_fusion.10
  426.1 1.6 add_select_fusion.10
  427.7 1.6 add_select_fusion.10
  429.4 1.6 add_select_fusion.10
  431.0 1.6 add_select_fusion.10
  432.6 1.6 add_select_fusion.10
  434.3 1.6 add_select_fusion.10
  435.9 1.6 add_select_fusion.10
  437.6 1.6 add_select_fusion.10
  439.2 1.9 reverse_add_fusion
  443.7 1.8 copy.79
  445.5 14.0 %fusion.6 = bf16[1,256,2240]{1,0,2:T(2,128)(2,1)S(1)} fusion(f32[1,256,2240]{1,0,2:T(1,128)S(1)} %bitcast.138, bf16[1,256,2240]{1,2,0:T(8,128)(2,1)S(1)} %copy-done.9), kind=kLoop, calls=%fused_computation.18 | loop fusion | flops 2293760 | bytes 4587520 | tf_op jit(solution)/shard_map/convert_element_type | solution.py:136
  (116 shorter events, 32.1 us)
Async XLA Ops:
  7.2 2.9 copy-start.8
  7.2 168.3 %all-gather.7.cloned.1.call-start = ((), (), s32[]{:S(2)}) async-start(), calls=%async_computation | async-start | bytes 19496960 | tf_op jit(solution)/shard_map/all_gather | solution.py:17
  10.0 23.8 %copy-start.4 = (bf16[2,128,20,112]{1,0,3,2:T(2,128)(2,1)}, bf16[2,128,20,112]{1,0,3,2:T(2,128)(2,1)S(1)}, u32[]{:S(2)}) copy-start(bf16[2,128,20,112]{1,0,3,2:T(2,128)(2,1)S(1)} %reshape.217) | copy-start | bytes 3440644
  30.5 46.1 %copy-start.1 = (bf16[2,128,20,112]{1,0,3,2:T(2,128)(2,1)}, bf16[2,128,20,112]{1,0,3,2:T(2,128)(2,1)S(1)}, u32[]{:S(2)}) copy-start(bf16[2,128,20,112]{1,0,3,2:T(2,128)(2,1)S(1)} %reshape.216) | copy-start | bytes 3440644
  33.8 368.3 %all-gather.9.cloned.1.call-start = ((), (), s32[]{:S(2)}) async-start(), calls=%async_computation.1 | async-start | bytes 19496960 | tf_op jit(solution)/shard_map/all_gather | solution.py:17
  33.9 190.2 %collective-permute-start.1 = (bf16[1,256,2240]{1,2,0:T(8,128)(2,1)}, bf16[1,256,2240]{1,2,0:T(8,128)(2,1)}, u32[]{:S(2)}, u32[]{:S(2)}) collective-permute-start(bf16[1,256,2240]{1,2,0:T(8,128)(2,1)} %param.12), channel_id=1, source_target_pairs={{1,0},{2,1},{3,2},{4,3},{5,4},{6,5},{7,6},{8,7},{9,8},{10,9},{11,1... | collective-permute-start | bytes 3440648 | tf_op jit(solution)/shard_map/ppermute | solution.py:35
  76.7 137.6 %copy-start.6 = (bf16[2,128,20,112]{1,0,3,2:T(2,128)(2,1)}, bf16[2,128,20,112]{1,0,3,2:T(2,128)(2,1)S(1)}, u32[]{:S(2)}) copy-start(bf16[2,128,20,112]{1,0,3,2:T(2,128)(2,1)S(1)} %reshape.218) | copy-start | bytes 3440644
  90.4 120.1 %copy-start.3 = (f32[2,20,112]{0,2,1:T(8,128)}, f32[2,20,112]{0,2,1:T(8,128)S(1)}, u32[]{:S(2)}) copy-start(f32[2,20,112]{0,2,1:T(8,128)S(1)} %reduce_window_sum.37) | copy-start | bytes 53764
  218.7 5.4 %copy-start.15 = (f32[2,2240]{1,0:T(2,128)S(1)}, f32[2,2240]{1,0:T(2,128)}, u32[]{:S(2)}) copy-start(f32[2,2240]{1,0:T(2,128)} %param.13) | copy-start | bytes 53764
  220.6 5.7 %copy-start.10 = (bf16[1,256,2240]{1,2,0:T(8,128)(2,1)}, bf16[1,256,2240]{1,2,0:T(8,128)(2,1)S(1)}, u32[]{:S(2)}) copy-start(bf16[1,256,2240]{1,2,0:T(8,128)(2,1)S(1)} %reshape.219) | copy-start | bytes 3440644
  220.6 28.9 %collective-permute-start = (bf16[1,256,2240]{1,2,0:T(8,128)(2,1)S(1)}, bf16[1,256,2240]{1,2,0:T(8,128)(2,1)S(1)}, u32[]{:S(2)}, u32[]{:S(2)}) collective-permute-start(bf16[1,256,2240]{1,2,0:T(8,128)(2,1)S(1)} %reshape.219), channel_id=1, source_target_pairs={{0,1},{1,2},{2,3},{3,4},{4,5},{5,6},{6,7},{7,8},{8,9},{9,10},{10,1... | collective-permute-start | bytes 3440648 | tf_op jit(solution)/shard_map/ppermute | solution.py:35
  254.3 2.2 copy-start
  269.2 3.0 copy-start.12
  269.2 3.7 copy-start.13
  269.2 3.7 copy-start.14
  274.6 1.8 copy-start.11
  290.5 1.6 copy-start.7
  439.2 2.0 copy-start.2
  441.1 1.5 copy-start.5
  443.7 1.8 copy-start.9
Sparse Core Ops, SparseCore 0:
  33.9 141.5 all-gather.6
  262.9 127.3 all-gather.8
where the time goes:
time: 479 us; the launch traced here: 470 us
  other arithmetic  165 us (34%)
  blocking collectives  127 us (27%)
  waiting for transfers between devices  79.1 us (17%)
  local copies, waits for them, and re-layouts  55.3 us (12%)
  matrix products  20.2 us (4%)
  between operations  14.7 us (3%)
  starting transfers between devices  7.86 us (2%)
    psum x1, blocking collectives, body(): lax.psum(local_conv, ('dp', 'seq')) / (clip_count * lax.axis_size('dp'))  79 us
    all_gather x2, waiting for transfers between devices, entering(): pieces = jax.tree.map(lambda part: lax.all_gather(part, axis), value)  55.9 us
    all_gather x2, blocking collectives, entering(): pieces = jax.tree.map(lambda part: lax.all_gather(part, axis), value)  48.5 us
    select_n x60, other arithmetic, step(): jnp.where(position < mine, new, old)  48.1 us
    ppermute x2, waiting for transfers between devices, from_behind(): return lax.ppermute(block, axis, route)  23.2 us
    max x1, other arithmetic, body(): q_feat = jnp.maximum(queries, 0).reshape(frame_shape)  18.7 us
    max x1, other arithmetic, body(): k_feat = jnp.maximum(keys, 0).reshape(frame_shape)  17.8 us
    reduce_sum x1, other arithmetic, body(): own_keys = jnp.sum(frame_keys, axis=1)  16.8 us
  transfers between devices with their start and end apart: 4, of which 2 were waited for; matrix products, arithmetic and copies ran while one was open for 29% of the time, Pallas kernels for 0%

commit v1 on v0

v1 whole, which is shorter than its diff:
```python
import functools

import jax
import jax.numpy as jnp
from jax import lax
from jax.experimental import pallas as pl
from jax.experimental.pallas import tpu as pltpu
from jax.sharding import PartitionSpec as P

HEADS = 20
HEAD_DIM = 112
FRAME = 128
LANES = 128
GROUP = 8
WIDTH = GROUP * HEAD_DIM
STEPS = -(-HEADS // GROUP)
LAST = HEADS - (STEPS - 1) * GROUP

denom_eps = 1e-06
loss_scale = 16.0
f32 = jnp.float32
bf16 = jnp.bfloat16


def lane_of(rows):
    return lax.broadcasted_iota(jnp.int32, (rows, LANES), 1)


def tile(ref, a, rows=slice(None)):
    return ref[rows, a * LANES : (a + 1) * LANES]


def take_head(ref, j, rows=slice(None)):
    if j == 0:
        return tile(ref, 0, rows)
    shift = (LANES - HEAD_DIM) * j
    if j == GROUP - 1:
        both = tile(ref, j - 1, rows)
    else:
        low, high = tile(ref, j - 1, rows), tile(ref, j, rows)
        both = jnp.where(lane_of(low.shape[0]) >= LANES - shift, low, high)
    return pltpu.roll(both, shift, 1)


def put_back(block, j):
    shift = (LANES - HEAD_DIM) * j
    return block if j == 0 else pltpu.roll(block, LANES - shift, 1)


def join_tiles(a, first, second):
    edge = HEAD_DIM - (LANES - HEAD_DIM) * a
    return jnp.where(lane_of(first.shape[0]) < edge, first, second)


def split(x):
    high = x.astype(bf16)
    return high, (x - high.astype(f32)).astype(bf16)


def dot(a, b, ca, cb):
    return lax.dot_general(a, b, (((ca,), (cb,)), ((), ())), preferred_element_type=f32)


def keep(x, fill=0.0):
    return jnp.where(lane_of(x.shape[0]) < HEAD_DIM, x, jnp.asarray(fill, x.dtype))


def with_one(x):
    lane = lane_of(x.shape[0])
    tail = jnp.where(lane == HEAD_DIM, 1.0, 0.0).astype(x.dtype)
    return jnp.where(lane < HEAD_DIM, x, tail)


def pad_rows(x):
    return jnp.concatenate([x, jnp.zeros((LANES - HEAD_DIM, x.shape[1]), x.dtype)], axis=0)


def each_head(work, flush):
    last = pl.program_id(0) == STEPS - 1

    @pl.when(jnp.logical_not(last))
    def _():
        flush([work(j) for j in range(GROUP)])

    @pl.when(last)
    def _():
        flush([work(j) for j in range(LAST)])


def write_tiles(ref, blocks, rows):
    n = len(blocks)
    for a in range(min(n, GROUP - 1)):
        second = blocks[a + 1] if a + 1 < n else blocks[a]
        ref[rows, a * LANES : (a + 1) * LANES] = join_tiles(a, blocks[a], second)


def state_kernel(k_ref, v_ref, tot_ref, first_ref):
    def work(j):
        k = jnp.maximum(take_head(k_ref, j), 0)
        v = with_one(take_head(v_ref, j))
        s0 = dot(k[:FRAME], v[:FRAME], 0, 0)[:HEAD_DIM]
        s1 = dot(k[FRAME:], v[FRAME:], 0, 0)[:HEAD_DIM]
        rows = slice(j * HEAD_DIM, (j + 1) * HEAD_DIM)
        first_ref[rows, :] = s0
        tot_ref[rows, :] = s0 + s1

    each_head(work, lambda _: None)


def scan_kernel(backward, x_ref, o_ref):
    n = x_ref.shape[0]
    order = range(n - 1, -1, -1) if backward else range(n)
    total = jnp.zeros(x_ref.shape[1:], f32)
    for i in order:
        o_ref[i] = total
        total = total + x_ref[i]


def middle_kernel(
    q_ref, cot_ref, next_ref, w_ref, prev_ref, tot_ref, first_ref,
    att_ref, gq_ref, gtot_ref, glast_ref, conv_ref, go_ref,
):
    frames = [slice(0, FRAME), slice(FRAME, 2 * FRAME)]
    for a in range(WIDTH // LANES):
        cols = slice(a * LANES, (a + 1) * LANES)
        c = [ref[r, cols].astype(f32) for ref in (cot_ref, next_ref) for r in frames]
        w0, w1 = w_ref[0:1, cols], w_ref[1:2, cols]
        for f in range(2):
            go_ref[frames[f], cols] = loss_scale * (c[f] + w0 * c[f + 1] + w1 * c[f + 2])

    def work(j):
        rows = slice(j * HEAD_DIM, (j + 1) * HEAD_DIM)
        q = keep(jnp.maximum(take_head(q_ref, j), 0))
        lane = lane_of(FRAME)
        atts, grads, gstates = [], [], []
        for f in range(2):
            own = (first_ref, tot_ref)[f]
            hi, lo = (pad_rows(x) for x in split(prev_ref[rows, :] + own[rows, :]))
            qf = q[frames[f]]
            num = dot(jnp.concatenate([qf, qf], 1), jnp.concatenate([hi, lo], 0), 1, 0)
            inv = 1.0 / (num[:, HEAD_DIM : HEAD_DIM + 1] + denom_eps)
            atts.append(put_back((num * inv).astype(bf16), j))
            gn = keep(take_head(go_ref, j, frames[f])) * inv
            gden = -inv * jnp.sum(gn * num, axis=1, keepdims=True)
            ghi, glo = split(jnp.where(lane == HEAD_DIM, gden, gn))
            gstates.append(
                dot(jnp.concatenate([qf, qf], 0), jnp.concatenate([ghi, glo], 0), 0, 0)[:HEAD_DIM]
            )
            gq = dot(
                jnp.concatenate([ghi, glo, ghi], 1), jnp.concatenate([hi, hi, lo], 1), 1, 1
            )
            gq = jnp.where(qf.astype(f32) > 0, gq, 0.0)
            grads.append(put_back(gq.astype(bf16), j))
        glast_ref[rows, :] = gstates[1]
        gtot_ref[rows, :] = gstates[0] + gstates[1]
        return atts, grads

    def flush(parts):
        for f in range(2):
            write_tiles(att_ref, [p[0][f] for p in parts], frames[f])
            write_tiles(gq_ref, [p[1][f] for p in parts], frames[f])

    each_head(work, flush)
    for a in range(WIDTH // LANES):
        cols = slice(a * LANES, (a + 1) * LANES)
        c = [ref[r, cols].astype(f32) for ref in (cot_ref, next_ref) for r in frames]
        att = [att_ref[r, cols].astype(f32) for r in frames]
        for i in range(2):
            conv_ref[i : i + 1, cols] = jnp.sum(
                att[0] * c[i + 1] + att[1] * c[i + 2], axis=0, keepdims=True
            )


def last_kernel(
    k_ref, v_ref, att_ref, back_ref, w_ref, next_ref, gtot_ref, glast_ref,
    mix_ref, gk_ref, gv_ref,
):
    frames = [slice(0, FRAME), slice(FRAME, 2 * FRAME)]

    def work(j):
        rows = slice(j * HEAD_DIM, (j + 1) * HEAD_DIM)
        k = keep(jnp.maximum(take_head(k_ref, j), 0))
        v = with_one(take_head(v_ref, j))
        gks, gvs = [], []
        for f in range(2):
            own = (gtot_ref, glast_ref)[f]
            hi, lo = (pad_rows(x) for x in split(next_ref[rows, :] + own[rows, :]))
            kf, vf = k[frames[f]], v[frames[f]]
            gv = dot(jnp.concatenate([kf, kf], 1), jnp.concatenate([hi, lo], 0), 1, 0)
            gk = dot(jnp.concatenate([vf, vf], 1), jnp.concatenate([hi, lo], 1), 1, 1)
            gk = jnp.where(kf.astype(f32) > 0, gk, 0.0)
            gvs.append(put_back(gv.astype(bf16), j))
            gks.append(put_back(gk.astype(bf16), j))
        return gks, gvs

    def flush(parts):
        for f in range(2):
            write_tiles(gk_ref, [p[0][f] for p in parts], frames[f])
            write_tiles(gv_ref, [p[1][f] for p in parts], frames[f])

    each_head(work, flush)
    for a in range(WIDTH // LANES):
        cols = slice(a * LANES, (a + 1) * LANES)
        c = [ref[r, cols].astype(f32) for ref in (back_ref, att_ref) for r in frames]
        w0, w1 = w_ref[0:1, cols], w_ref[1:2, cols]
        for f in range(2):
            mix_ref[frames[f], cols] = (c[f + 2] + w0 * c[f + 1] + w1 * c[f]).astype(bf16)


def call(kernel, name, outs, *args, scratch=(), cost=None):
    tok = pl.BlockSpec((2 * FRAME, WIDTH), lambda g: (0, g))
    state = pl.BlockSpec((WIDTH, LANES), lambda g: (g, 0))
    pair = pl.BlockSpec((2, WIDTH), lambda g: (0, g))

    def spec(x):
        return pair if x.shape[0] == 2 else (state if x.shape[1] == LANES else tok)

    return pl.pallas_call(
        kernel,
        grid=(STEPS,),
        in_specs=[spec(a) for a in args],
        out_specs=[spec(o) for o in outs],
        out_shape=outs,
        scratch_shapes=list(scratch),
        compiler_params=pltpu.CompilerParams(vmem_limit_bytes=40 * 2**20),
        name=name,
    )(*args)


def exclusive_sum(x, axis, backward):
    n = lax.axis_size(axis)
    pieces = x.reshape(n, x.shape[0] // n, LANES)
    pieces = lax.all_to_all(pieces, axis, 0, 0, tiled=True)
    sums = pl.pallas_call(
        functools.partial(scan_kernel, backward),
        out_shape=jax.ShapeDtypeStruct(pieces.shape, f32),
        compiler_params=pltpu.CompilerParams(vmem_limit_bytes=40 * 2**20),
        name="scan",
    )(pieces)
    return lax.all_to_all(sums, axis, 0, 0, tiled=True).reshape(x.shape)


def from_behind(block, axis, distance):
    devices = range(lax.axis_size(axis))
    route = [(i - distance, i) for i in devices if i - distance in devices]
    return lax.ppermute(block, axis, route)


def body(queries, keys, values, cotangent, conv_weight):
    clips, toks, width = queries.shape
    q, k, v, cot = (x.reshape(toks, width) for x in (queries, keys, values, cotangent))
    n = lax.axis_size("seq")
    unit = 16 * n
    rows = -(-HEADS * HEAD_DIM // unit) * unit
    state = jax.ShapeDtypeStruct((rows, LANES), f32)
    tokens = jax.ShapeDtypeStruct((toks, width), bf16)

    cot_next = from_behind(cot, "seq", -1)
    tot, first = call(state_kernel, "states", [state, state], k, v)
    prev = exclusive_sum(tot, "seq", False)
    att, gq, gtot, glast, conv = call(
        middle_kernel, "middle",
        [tokens, tokens, state, state, jax.ShapeDtypeStruct((2, width), f32)],
        q, cot, cot_next, conv_weight, prev, tot, first,
        scratch=[pltpu.VMEM((2 * FRAME, WIDTH), f32)],
    )
    back = from_behind(att, "seq", 1)
    conv = jnp.sum(lax.all_gather(conv, "seq"), 0)
    conv = jnp.sum(lax.all_gather(conv, "dp"), 0) / (clips * lax.axis_size("dp"))
    follow = exclusive_sum(gtot, "seq", True)
    mixed, gk, gv = call(
        last_kernel, "last", [tokens] * 3, k, v, att, back, conv_weight, follow, gtot, glast
    )
    return tuple(x.reshape(clips, toks, width) for x in (mixed, gq, gk, gv)) + (conv,)


def solution(mesh):
    blocks = P("dp", "seq", None)
    return jax.shard_map(
        body,
        mesh=mesh,
        in_specs=(blocks,) * 4 + (P(),),
        out_specs=(blocks,) * 4 + (P(),),
        check_vma=False,
    )
```

time: 479 us -> 234 us (0.49); the launches traced: 470 us -> 231 us
  other arithmetic: 165 us -> 4.66 us
  blocking collectives: 127 us -> 65.2 us
  Pallas kernels: 0 us -> 31.9 us
  waiting for transfers between devices: 79.1 us -> 51.7 us
  starting transfers between devices: 7.86 us -> 31.3 us
  matrix products: 20.2 us -> 0 us
  between operations: 14.7 us -> 0.79 us
  local copies, waits for them, and re-layouts: 55.3 us -> 45.6 us
    psum x1 -> x0, blocking collectives: 79 us -> none  [body(): lax.psum(local_conv, ('dp', 'seq')) / (clip_count * lax.axis_size('dp'))]
    all_gather x2 -> x0, waiting for transfers between devices: 55.9 us -> none  [entering(): pieces = jax.tree.map(lambda part: lax.all_gather(part, axis), value)]
    select_n x60 -> x0, other arithmetic: 48.1 us -> none  [step(): jnp.where(position < mine, new, old)]
    all_to_all x0 -> x4, waiting for transfers between devices: none -> 37.1 us  [the longest x2 28.3 us: exclusive_sum(): pieces = lax.all_to_all(pieces, axis, 0, 0, tiled=True)]
    max x2 -> x0, other arithmetic: 36.5 us -> none  [the longest x1 18.7 us: body(): q_feat = jnp.maximum(queries, 0).reshape(frame_shape)]
    unnamed x35 -> x60, local copies, waits for them, and re-layouts: 3.79 us -> 39.5 us
    pallas_call x0 -> x5, Pallas kernels: none -> 31.9 us  [the longest x3 30.5 us: call(): pl.pallas_call(kernel, grid=(STEPS,), in_specs=[spec(a) for a in args], o...]
    convert_element_type x3 -> x0, other arithmetic: 30.3 us -> none  [the longest x1 14.1 us: body(): jnp.where(queries > 0, grad_q.reshape(out_shape), 0.0).astype(jnp.bfloat16)]
  transfers between devices with their start and end apart: 4 -> 6, of which waited for: 2 -> 4; matrix products, arithmetic and copies ran while one was open for 29% -> 8% of each run, Pallas kernels for 0% -> 1%
where the time goes in v1:
time: 234 us; the launch traced here: 231 us
  blocking collectives  65.2 us (28%)
  waiting for transfers between devices  51.7 us (22%)
  local copies, waits for them, and re-layouts  45.6 us (19%)
  Pallas kernels  31.9 us (14%)
  starting transfers between devices  31.3 us (13%)
  other arithmetic  4.66 us (2%)
    all_gather x1, blocking collectives, body(): conv = jnp.sum(lax.all_gather(conv, 'seq'), 0)  42.8 us
    unnamed x60, local copies, waits for them, and re-layouts  39.5 us
    pallas_call x3, Pallas kernels, call(): pl.pallas_call(kernel, grid=(STEPS,), in_specs=[spec(a) for a in args], o...  30.5 us
    all_to_all x2, waiting for transfers between devices, exclusive_sum(): pieces = lax.all_to_all(pieces, axis, 0, 0, tiled=True)  28.3 us
    all_gather x1, blocking collectives, body(): lax.all_gather(conv, 'dp')  22.4 us
    ppermute x2, waiting for transfers between devices, from_behind(): return lax.ppermute(block, axis, route)  14.5 us
    all_to_all x2, starting transfers between devices, exclusive_sum(): pieces = lax.all_to_all(pieces, axis, 0, 0, tiled=True)  13.8 us
    all_to_all x2, starting transfers between devices, exclusive_sum(): return lax.all_to_all(sums, axis, 0, 0, tiled=True).reshape(x.shape)  12.1 us
  transfers between devices with their start and end apart: 6, of which 4 were waited for; matrix products, arithmetic and copies ran while one was open for 8% of the time, Pallas kernels for 1%

profile of v1, /device:TPU:2, one launch (start us, length us, event | category | flops | bytes accessed | tf_op | source)
XLA Modules:
  0.0 231.2 jit_solution(16437650305777930395)
XLA Ops:
  0.6 0.0 copy-start.25
  0.6 1.7 copy.18
  2.3 0.0 copy-done.25
  2.3 0.7 copy.19
  3.0 3.7 %states.1 = (f32[2304,128]{1,0:T(8,128)S(1)}, f32[2304,128]{1,0:T(8,128)S(1)}) custom-call(bf16[256,2240]{1,0:T(8,128)(2,1)S(1)} %bitcast.15, bf16[256,2240]{1,0:T(8,128)(2,1)S(1)} %bitcast.17), custom_call_target="tpu_custom_call" | custom-call | tf_op jit(solution)/shard_map/states/pallas_call | solution.py:218
  6.7 0.0 copy-start.5
  6.7 1.0 copy-done.5
  7.8 1.0 copy-done.20
  8.8 7.5 %all-to-all-start = ((f32[16,144,128]{2,1,0:T(8,128)}), f32[16,144,128]{2,1,0:T(8,128)S(1)}, u32[]{:S(2)}, u32[]{:S(2)}) async-start(f32[16,144,128]{2,1,0:T(8,128)} %bitcast.20), calls=%async_computation | async-start | bytes 2359296 | tf_op jit(solution)/shard_map/all_to_all | solution.py:233
  16.3 2.0 collective-permute-start
  18.3 16.6 %all-to-all-done.x_ref = f32[16,144,128]{2,1,0:T(8,128)S(1)} async-done(((f32[16,144,128]{2,1,0:T(8,128)}), f32[16,144,128]{2,1,0:T(8,128)S(1)}, u32[]{:S(2)}, u32[]{:S(2)}) %all-to-all-start) | async-done | bytes 1179680 | tf_op jit(solution)/shard_map/all_to_all | solution.py:233
  34.9 0.1 scan.2
  35.0 0.0 copy-start.4
  35.0 1.0 copy-done.4
  36.0 4.2 %all-to-all-start.1 = ((f32[16,144,128]{2,1,0:T(8,128)}), f32[16,144,128]{2,1,0:T(8,128)S(1)}, u32[]{:S(2)}, u32[]{:S(2)}) async-start(f32[16,144,128]{2,1,0:T(8,128)} %copy-done.4), calls=%async_computation.1 | async-start | bytes 2359296 | tf_op jit(solution)/shard_map/all_to_all | solution.py:240
  40.2 2.4 %copy.21 = bf16[1,256,2240]{2,1,0:T(8,128)(2,1)} copy(bf16[1,256,2240]{1,2,0:T(8,128)(2,1)} %param.8) | data formatting | bytes 2293760 | tf_op args[3]
  42.6 2.4 %copy.20 = bf16[1,256,2240]{2,1,0:T(8,128)(2,1)} copy(bf16[1,256,2240]{1,2,0:T(8,128)(2,1)} %param.5) | data formatting | bytes 2293760 | tf_op args[0]
  45.0 14.5 %collective-permute-done = bf16[256,2240]{0,1:T(8,128)(2,1)} collective-permute-done((bf16[256,2240]{0,1:T(8,128)(2,1)}, bf16[256,2240]{0,1:T(8,128)(2,1)}, u32[]{:S(2)}, u32[]{:S(2)}) %collective-permute-start) | collective-permute-done | bytes 1146912 | tf_op jit(solution)/shard_map/ppermute | solution.py:246
  59.5 2.4 %copy.23.next_ref = bf16[256,2240]{1,0:T(8,128)(2,1)} copy(bf16[256,2240]{0,1:T(8,128)(2,1)} %collective-permute-done) | data formatting | bytes 2293760 | tf_op jit(solution)/shard_map/ppermute | solution.py:246
  61.9 8.9 %all-to-all-done.1 = f32[16,144,128]{2,1,0:T(8,128)S(1)} async-done(((f32[16,144,128]{2,1,0:T(8,128)}), f32[16,144,128]{2,1,0:T(8,128)S(1)}, u32[]{:S(2)}, u32[]{:S(2)}) %all-to-all-start.1) | async-done | bytes 1179680 | tf_op jit(solution)/shard_map/all_to_all | solution.py:240
  70.7 1.0 copy-done.7
  71.8 1.3 copy-done.6
  73.0 1.3 copy-done.8
  74.3 1.3 copy-done.9
  75.6 1.3 copy-done.10
  76.8 1.3 copy-done.11
  78.1 1.3 copy-done.21
  79.4 0.7 copy-done.22
  80.1 21.9 %middle.1 = (bf16[256,2240]{1,0:T(8,128)(2,1)S(1)}, bf16[256,2240]{1,0:T(8,128)(2,1)S(1)}, f32[2304,128]{1,0:T(8,128)S(1)}, f32[2304,128]{1,0:T(8,128)S(1)}, f32[2,2240]{1,0:T(2,128)S(1)}) custom-call(bf16[256,2240]{1,0:T(8,128)(2,1)S(1)} %bitcast.23, bf16[256,2240]{1,0:T(8,128)(2,1)S(1)} %bitcast.22, bf16[256,2240]{1,0:T(8,128)(2,1)S(1)} %copy-done.11, ...), custom_call_target="tpu_custom_call" | custom-call | tf_op jit(solution)/shard_map/middle/pallas_call | solution.py:218
  102.0 0.0 copy-start
  102.0 1.0 copy-done
  103.0 1.0 copy-done.12
  104.1 1.0 copy-done.14
  105.1 0.6 copy-done.24
  105.7 6.3 %all-to-all-start.2 = ((f32[16,144,128]{2,1,0:T(8,128)}), f32[16,144,128]{2,1,0:T(8,128)}, u32[]{:S(2)}, u32[]{:S(2)}) async-start(f32[16,144,128]{2,1,0:T(8,128)} %bitcast.19), calls=%async_computation.2 | async-start | bytes 2359296 | tf_op jit(solution)/shard_map/all_to_all | solution.py:233
  112.0 1.4 copy.24
  113.4 3.4 %collective-permute-start.1 = (bf16[256,2240]{0,1:T(8,128)(2,1)}, bf16[256,2240]{0,1:T(8,128)(2,1)}, u32[]{:S(2)}, u32[]{:S(2)}) collective-permute-start(bf16[256,2240]{0,1:T(8,128)(2,1)} %copy.24), channel_id=1, source_target_pairs={{0,1},{1,2},{2,3},{3,4},{4,5},{5,6},{6,7},{7,8},{8,9},{9,10},{10,1... | collective-permute-start | bytes 3440648 | tf_op jit(solution)/shard_map/ppermute | solution.py:246
  116.8 11.7 %all-to-all-done.2.x_ref = f32[16,144,128]{2,1,0:T(8,128)} async-done(((f32[16,144,128]{2,1,0:T(8,128)}), f32[16,144,128]{2,1,0:T(8,128)}, u32[]{:S(2)}, u32[]{:S(2)}) %all-to-all-start.2) | async-done | bytes 1179680 | tf_op jit(solution)/shard_map/all_to_all | solution.py:233
  128.4 1.3 scan.3
  129.8 0.0 copy-start.3
  129.8 1.0 copy-done.3
  130.8 7.9 %all-to-all-start.3 = ((f32[16,144,128]{2,1,0:T(8,128)}), f32[16,144,128]{2,1,0:T(8,128)}, u32[]{:S(2)}, u32[]{:S(2)}) async-start(f32[16,144,128]{2,1,0:T(8,128)} %copy-done.3), calls=%async_computation.3 | async-start | bytes 2359296 | tf_op jit(solution)/shard_map/all_to_all | solution.py:240
  138.7 2.4 %copy.27 = bf16[1,256,2240]{1,2,0:T(8,128)(2,1)} copy(bf16[1,256,2240]{2,1,0:T(8,128)(2,1)} %bitcast.24) | data formatting | bytes 2293760
  141.1 42.8 %all-gather.2 = f32[16,2,2240]{2,1,0:T(2,128)} all-gather(f32[1,2,2240]{2,1,0:T(2,128)} %bitcast.28), channel_id=2, replica_groups=mesh['dp'=16,'seq'=16] {'seq'}, dimensions={0}, use_global_device_ids=true | all-gather | bytes 304640 | tf_op jit(solution)/shard_map/all_gather | solution.py:268
  183.9 1.7 reduce_sum.18
  185.6 22.4 %all-gather.3 = f32[16,2,2240]{2,1,0:T(2,128)} all-gather(f32[1,2,2240]{2,1,0:T(2,128)} %bitcast.30), channel_id=3, replica_groups=mesh['dp'=16,'seq'=16] {'dp'}, dimensions={0}, use_global_device_ids=true | all-gather | bytes 304640 | tf_op jit(solution)/shard_map/all_gather | solution.py:269
  208.0 1.7 reduce_sum.19
  209.6 1.3 broadcast_multiply_fusion
  211.0 0.0 collective-permute-done.1
  211.0 2.4 %copy.25.back_ref = bf16[256,2240]{1,0:T(8,128)(2,1)} copy(bf16[256,2240]{0,1:T(8,128)(2,1)} %collective-permute-done.1) | data formatting | bytes 2293760 | tf_op jit(solution)/shard_map/ppermute | solution.py:246
  213.3 0.0 all-to-all-done.3
  213.3 1.3 copy-done.1
  214.6 1.3 copy-done.2
  215.9 1.3 copy-done.13
  217.2 0.7 copy-done.23
  217.9 4.9 %last.1 = (bf16[256,2240]{1,0:T(8,128)(2,1)S(1)}, bf16[256,2240]{1,0:T(8,128)(2,1)S(1)}, bf16[256,2240]{1,0:T(8,128)(2,1)S(1)}) custom-call(bf16[256,2240]{1,0:T(8,128)(2,1)S(1)} %bitcast.16, bf16[256,2240]{1,0:T(8,128)(2,1)S(1)} %bitcast.18, bf16[256,2240]{1,0:T(8,128)(2,1)S(1)} %get-tuple-element.17.att_ref, bf16[256,2240]{1,0:T(8,128)(2,1)S(1)} %copy-done.2, ...), custom_call_target="tpu_custom_call" | custom-call | tf_op jit(solution)/shard_map/last/pallas_call | solution.py:218
  222.8 0.0 copy-start.15
  222.8 1.0 copy-done.15
  223.9 1.0 copy-done.17
  224.9 1.0 copy-done.19
  225.9 2.5 %copy.26 = bf16[1,256,2240]{1,2,0:T(8,128)(2,1)} copy(bf16[1,256,2240]{2,1,0:T(8,128)(2,1)} %bitcast.27) | data formatting | bytes 2293760
  228.4 0.0 copy-done.18
  228.4 1.4 copy.28
  229.8 1.4 copy.29
  (21 shorter events, 0.0 us)
Async XLA Ops:
  0.6 1.7 copy-start.25
  6.7 1.0 copy-start.5
  7.8 1.0 copy-start.20
  8.8 26.1 %all-to-all-start = ((f32[16,144,128]{2,1,0:T(8,128)}), f32[16,144,128]{2,1,0:T(8,128)S(1)}, u32[]{:S(2)}, u32[]{:S(2)}) async-start(f32[16,144,128]{2,1,0:T(8,128)} %bitcast.20), calls=%async_computation | async-start | bytes 2359296 | tf_op jit(solution)/shard_map/all_to_all | solution.py:233
  16.3 43.2 %collective-permute-start = (bf16[256,2240]{0,1:T(8,128)(2,1)}, bf16[256,2240]{0,1:T(8,128)(2,1)}, u32[]{:S(2)}, u32[]{:S(2)}) collective-permute-start(bf16[256,2240]{0,1:T(8,128)(2,1)} %bitcast.29), channel_id=1, source_target_pairs={{1,0},{2,1},{3,2},{4,3},{5,4},{6,5},{7,6},{8,7},{9,8},{10,9},{11,1... | collective-permute-start | bytes 3440648 | tf_op jit(solution)/shard_map/ppermute | solution.py:246
  35.0 1.0 copy-start.4
  36.0 34.7 %all-to-all-start.1 = ((f32[16,144,128]{2,1,0:T(8,128)}), f32[16,144,128]{2,1,0:T(8,128)S(1)}, u32[]{:S(2)}, u32[]{:S(2)}) async-start(f32[16,144,128]{2,1,0:T(8,128)} %copy-done.4), calls=%async_computation.1 | async-start | bytes 2359296 | tf_op jit(solution)/shard_map/all_to_all | solution.py:240
  70.7 1.0 copy-start.7
  71.8 1.3 copy-start.6
  73.0 1.3 copy-start.8
  74.3 1.3 copy-start.9
  75.6 1.3 copy-start.10
  76.8 1.3 copy-start.11
  78.1 1.3 copy-start.21
  79.4 0.7 copy-start.22
  102.0 1.0 copy-start
  103.0 1.0 copy-start.12
  104.1 1.0 copy-start.14
  105.1 0.6 copy-start.24
  105.7 22.7 %all-to-all-start.2 = ((f32[16,144,128]{2,1,0:T(8,128)}), f32[16,144,128]{2,1,0:T(8,128)}, u32[]{:S(2)}, u32[]{:S(2)}) async-start(f32[16,144,128]{2,1,0:T(8,128)} %bitcast.19), calls=%async_computation.2 | async-start | bytes 2359296 | tf_op jit(solution)/shard_map/all_to_all | solution.py:233
  113.4 97.6 %collective-permute-start.1 = (bf16[256,2240]{0,1:T(8,128)(2,1)}, bf16[256,2240]{0,1:T(8,128)(2,1)}, u32[]{:S(2)}, u32[]{:S(2)}) collective-permute-start(bf16[256,2240]{0,1:T(8,128)(2,1)} %copy.24), channel_id=1, source_target_pairs={{0,1},{1,2},{2,3},{3,4},{4,5},{5,6},{6,7},{7,8},{8,9},{9,10},{10,1... | collective-permute-start | bytes 3440648 | tf_op jit(solution)/shard_map/ppermute | solution.py:246
  129.8 1.0 copy-start.3
  130.8 82.5 %all-to-all-start.3 = ((f32[16,144,128]{2,1,0:T(8,128)}), f32[16,144,128]{2,1,0:T(8,128)}, u32[]{:S(2)}, u32[]{:S(2)}) async-start(f32[16,144,128]{2,1,0:T(8,128)} %copy-done.3), calls=%async_computation.3 | async-start | bytes 2359296 | tf_op jit(solution)/shard_map/all_to_all | solution.py:240
  213.3 1.3 copy-start.1
  214.6 1.3 copy-start.2
  215.9 1.3 copy-start.13
  217.2 0.7 copy-start.23
  222.8 1.0 copy-start.15
  223.9 1.0 copy-start.17
  224.9 1.0 copy-start.19
  225.9 2.5 %copy-start.18 = (bf16[256,2240]{1,0:T(8,128)(2,1)S(1)}, bf16[256,2240]{1,0:T(8,128)(2,1)}, u32[]{:S(2)}) copy-start(bf16[256,2240]{1,0:T(8,128)(2,1)} %copy-done.17) | copy-start | bytes 3440644
  228.4 1.4 copy-start.16

commit v2 on v0

v2 whole, which is shorter than its diff:
```python
import functools

import jax
import jax.numpy as jnp
from jax import lax
from jax.experimental import pallas as pl
from jax.experimental.pallas import tpu as pltpu
from jax.sharding import PartitionSpec as P

HEADS = 20
HEAD_DIM = 112
FRAME = 128
LANES = 128
HALF = HEADS // 2
HALF_ROWS = HALF * HEAD_DIM
PIECE = 16
TOLD = 48
WIRE = jnp.bfloat16
SCAN_STEPS = 1

denom_eps = 1e-06
loss_scale = 16.0
f32 = jnp.float32
bf16 = jnp.bfloat16

PARAMS = pltpu.CompilerParams(vmem_limit_bytes=56 * 2**20)
frames = [slice(0, FRAME), slice(FRAME, 2 * FRAME)]
units = [(j, f) for j in range(HALF) for f in range(2)]


def shape(*dims, dtype=f32):
    return jax.ShapeDtypeStruct(dims, dtype)


def split(x):
    high = x.astype(bf16)
    return high, (x - high.astype(f32)).astype(bf16)


def dot(a, b, ca, cb):
    return lax.dot_general(a, b, (((ca,), (cb,)), ((), ())), preferred_element_type=f32)


def cat(parts, axis):
    return jnp.concatenate(parts, axis=axis)


def first_of_pad(columns):
    return lax.broadcasted_iota(jnp.int32, (LANES - HEAD_DIM, columns), 0) == 0


def with_one(v):
    return cat([v, jnp.where(first_of_pad(v.shape[1]), 1.0, 0.0).astype(bf16)], 0)


def rows_of(j):
    return slice(j * HEAD_DIM, (j + 1) * HEAD_DIM)


def filtered(c, w_ref, rows):
    w0, w1 = w_ref[rows, 0:1], w_ref[rows, 1:2]
    return c[0] + w0 * c[1] + w1 * c[2]


def parts_of(rows, *refs):
    return [ref[rows, fr].astype(f32) for ref in refs for fr in frames]


def grid_of(rows):
    dims = (rows // PIECE, PIECE, LANES)
    return [lax.broadcasted_iota(jnp.int32, dims, d) for d in (2, 1)]


def slots():
    channel = lax.broadcasted_iota(jnp.int32, (LANES, LANES), 0)
    column = lax.broadcasted_iota(jnp.int32, (LANES, LANES), 1)
    hit = (channel < HEAD_DIM) & (column - (HEAD_DIM + 2) == channel // PIECE)
    return jnp.where(hit, 1.0, 0.0).astype(bf16)


def encode(x):
    lane, row = grid_of(x.shape[0])
    x3 = x.reshape(lane.shape)
    sums = jnp.sum(x3, axis=1, keepdims=True)
    mean = sums / (sums[:, :, HEAD_DIM : HEAD_DIM + 1] + 1e-30)
    mean = jnp.where(lane[:, :1] < HEAD_DIM, mean, 0.0).astype(bf16).astype(f32)
    key_sum = x3[:, :, HEAD_DIM : HEAD_DIM + 1]
    low = key_sum - key_sum.astype(bf16).astype(f32)
    y = jnp.where(lane == HEAD_DIM + 1, low, x3 - key_sum * mean)
    kept = jnp.where(lane % PIECE == row, mean, 0.0).reshape(x.shape).astype(bf16)
    return (y.reshape(x.shape) + dot(kept, slots(), 1, 0)).astype(WIRE)


def decode(y):
    lane, row = grid_of(y.shape[0])
    column = lax.broadcasted_iota(jnp.int32, (LANES, LANES), 1)
    pair = (column == HEAD_DIM) | (column == HEAD_DIM + 1)
    pair = jnp.where(pair, 1.0, 0.0).astype(bf16)
    both = dot(y, cat([slots(), pair], 0), 1, 1)
    key_sum = both[:, LANES:].reshape(lane.shape)
    mean = jnp.where(lane % PIECE == row, both[:, :LANES].reshape(lane.shape), 0.0)
    mean = jnp.sum(mean, axis=1, keepdims=True)
    x = y.astype(f32).reshape(lane.shape) + key_sum * mean
    x = jnp.where(lane < HEAD_DIM, x, jnp.where(lane == HEAD_DIM, key_sum, 0.0))
    return x.reshape(y.shape)


def encode_grad(x):
    lane = lax.broadcasted_iota(jnp.int32, x.shape, 1)
    low = pltpu.roll(x - x.astype(bf16).astype(f32), 1, 1)
    return jnp.where(lane == HEAD_DIM + 1, low, x).astype(WIRE)


def decode_grad(y):
    lane = lax.broadcasted_iota(jnp.int32, y.shape, 1)
    x = y.astype(f32)
    whole = x + pltpu.roll(x, LANES - 1, 1)
    return jnp.where(lane < HEAD_DIM, x, jnp.where(lane == HEAD_DIM, whole, 0.0))


def state_kernel(k_ref, v_ref, tot_ref, first_ref, send_ref):
    ks = [jnp.maximum(k_ref[rows_of(j), :], 0) for j in range(HALF)]
    vs = [with_one(v_ref[rows_of(j), :]) for j in range(HALF)]
    firsts = [dot(k[:, :FRAME], v[:, :FRAME], 1, 1) for k, v in zip(ks, vs)]
    seconds = [dot(k[:, FRAME:], v[:, FRAME:], 1, 1) for k, v in zip(ks, vs)]
    for j in range(HALF):
        tot = firsts[j] + seconds[j]
        first_ref[rows_of(j), :] = firsts[j]
        tot_ref[rows_of(j), :] = tot
        send_ref[rows_of(j), :] = encode(tot)


def scan_kernel(x_ref, o_ref):
    parts = [decode(x_ref[i]) for i in range(x_ref.shape[0])]
    totals = [jnp.zeros_like(parts[0])]
    for part in parts[:-1]:
        totals.append(totals[-1] + part)
    for i, total in enumerate([encode(total) for total in totals]):
        o_ref[i] = total


def scan_back_kernel(x_ref, o_ref, sum_ref):
    n, rows = o_ref.shape[:2]
    parts = [decode_grad(x_ref[i, :rows]) for i in range(n)]
    totals = [jnp.zeros_like(parts[0])]
    for part in parts[:0:-1]:
        totals.append(totals[-1] + part)
    for i, total in enumerate([encode_grad(total) for total in totals]):
        o_ref[n - 1 - i] = total
    sum_ref[...] = sum(x_ref[i, rows:].astype(f32) for i in range(n))


def numerators(qs, states):
    nums = {u: dot(cat(states[u], 0), cat([qs[u]] * 2, 0), 0, 0) for u in qs}
    invs = {u: 1.0 / (num[HEAD_DIM : HEAD_DIM + 1] + denom_eps) for u, num in nums.items()}
    return {u: num[:HEAD_DIM] for u, num in nums.items()}, invs


def gradients(go, num, inv):
    gn = go * inv
    gden = -inv * jnp.sum(gn * num, axis=0, keepdims=True)
    return split(cat([gn, jnp.where(first_of_pad(FRAME), gden, 0.0)], 0))


def middle_kernel(
    chunk, q_ref, behind_ref, cot_ref, ahead_ref, w_ref, prev_ref, tot_ref, first_ref,
    att0_ref, att1_ref, att_behind_ref, gtot_ref, glast_ref, send_ref, conv_ref,
):
    step = pl.program_id(0)
    stride = chunk + TOLD
    qs, states, cots, gos = {}, {}, {}, {}
    for j in range(HALF):
        rows = rows_of(j)
        q = jnp.maximum(q_ref[rows, :], 0)
        before = decode(prev_ref[rows, :])
        qs[j, -1] = jnp.maximum(behind_ref[rows, :], 0)
        states[j, -1] = split(before)
        for f in range(2):
            qs[j, f] = q[:, frames[f]]
            states[j, f] = split(before + (first_ref, tot_ref)[f][rows, :])
        w0, w1 = w_ref[rows, 0:1], w_ref[rows, 1:2]
        c0, c1 = parts_of(rows, cot_ref)
        c2 = ahead_ref[rows, :].astype(f32)
        cots[j] = c0, c1, c2
        gos[j, -1] = loss_scale * (w1 * c1)
        gos[j, 0] = loss_scale * (c0 + w0 * c1 + w1 * c2)
        gos[j, 1] = loss_scale * (c1 + w0 * c2)
    nums, invs = numerators(qs, states)
    atts = {u: (nums[u] * invs[u]).astype(bf16) for u in qs}
    grads = {u: gradients(gos[u], nums[u], invs[u]) for u in qs}
    gstates = {u: dot(cat([qs[u]] * 2, 1), cat(grads[u], 1), 1, 1) for u in qs}
    for j in range(HALF):
        rows = rows_of(j)
        own = gstates[j, 0] + gstates[j, 1]
        glast_ref[rows, :] = gstates[j, 1]
        gtot_ref[rows, :] = own
        wire = encode_grad(own + gstates[j, -1])
        for at in range(rows.start, rows.stop, PIECE):
            to = step * (send_ref.shape[0] // 2) + at // chunk * stride + at % chunk
            piece = wire[at - rows.start : at - rows.start + PIECE]
            send_ref[pl.ds(pl.multiple_of(to, PIECE), PIECE), :] = piece
        att_behind_ref[rows, :], att0_ref[rows, :], att1_ref[rows, :] = (
            atts[j, f] for f in (-1, 0, 1)
        )
        wide = [atts[j, f].astype(f32) for f in (-1, 0)]
        c0, c1, c2 = cots[j]
        for i, part in enumerate([wide[0] * c0 + wide[1] * c1, wide[0] * c1 + wide[1] * c2]):
            line = jnp.sum(part.T, axis=0, keepdims=True)
            line = cat([line, jnp.zeros((1, LANES - HEAD_DIM), f32)], 1)
            conv_ref[pl.ds(i * HEADS + step * HALF + j, 1), :] = line

    @pl.when(step == 1)
    def _():
        conv_ref[2 * HEADS :, :] = jnp.zeros((TOLD - 2 * HEADS, LANES), f32)
        conv = conv_ref[...].astype(send_ref.dtype)
        for i in range(send_ref.shape[0] // stride):
            send_ref[i * stride + chunk : (i + 1) * stride, :] = conv


def queries_kernel(
    q_ref, cot_ref, ahead_ref, ahead2_ref, w_ref, prev_ref, tot_ref, first_ref, gq_ref
):
    qs, states, gos = {}, {}, {}
    for j in range(HALF):
        rows = rows_of(j)
        q = jnp.maximum(q_ref[rows, :], 0)
        before = decode(prev_ref[rows, :])
        c = parts_of(rows, cot_ref) + [r[rows, :].astype(f32) for r in (ahead_ref, ahead2_ref)]
        for f in range(2):
            qs[j, f] = q[:, frames[f]]
            states[j, f] = split(before + (first_ref, tot_ref)[f][rows, :])
            gos[j, f] = loss_scale * filtered(c[f : f + 3], w_ref, rows)
    nums, invs = numerators(qs, states)
    for j, f in qs:
        u = j, f
        (hi, lo), (ghi, glo) = states[u], gradients(gos[u], nums[u], invs[u])
        gq = dot(cat([hi, hi, lo], 1), cat([ghi, glo, ghi], 0), 1, 0)
        gq = jnp.where(qs[u].astype(f32) > 0, gq, 0.0)
        gq_ref[rows_of(j), frames[f]] = gq.astype(bf16)


def mixed_kernel(att0_ref, att1_ref, behind_ref, behind2_ref, w_ref, mix_ref):
    for j in range(HALF):
        rows = rows_of(j)
        c = [r[rows, :].astype(f32) for r in (behind2_ref, behind_ref, att0_ref, att1_ref)]
        for f in range(2):
            mix_ref[rows, frames[f]] = filtered(c[f : f + 3][::-1], w_ref, rows).astype(bf16)


def last_kernel(k_ref, v_ref, follow_ref, gtot_ref, glast_ref, gk_ref, gv_ref):
    ks, vs, states = {}, {}, {}
    for j in range(HALF):
        rows = rows_of(j)
        k = jnp.maximum(k_ref[rows, :], 0)
        v = with_one(v_ref[rows, :])
        behind = decode_grad(follow_ref[rows, :])
        for f in range(2):
            ks[j, f], vs[j, f] = k[:, frames[f]], v[:, frames[f]]
            states[j, f] = split(behind + (gtot_ref, glast_ref)[f][rows, :])
    gvs = {u: dot(cat(states[u], 0), cat([ks[u]] * 2, 0), 0, 0) for u in units}
    gks = {u: dot(cat(states[u], 1), cat([vs[u]] * 2, 0), 1, 0) for u in units}
    for j, f in units:
        rows = rows_of(j)
        gv_ref[rows, frames[f]] = gvs[j, f][:HEAD_DIM].astype(bf16)
        gk = jnp.where(ks[j, f].astype(f32) > 0, gks[j, f], 0.0)
        gk_ref[rows, frames[f]] = gk.astype(bf16)


def call(kernel, name, outs, *args, whole=()):
    def spec(x):
        if any(x is w for w in whole):
            return pl.BlockSpec(x.shape, lambda g: (0, 0))
        return pl.BlockSpec((x.shape[0] // 2, x.shape[1]), lambda g: (g, 0))

    return pl.pallas_call(
        kernel,
        grid=(2,),
        in_specs=[spec(a) for a in args],
        out_specs=[spec(o) for o in outs],
        out_shape=outs,
        compiler_params=PARAMS,
        name=name,
    )(*args)


def scan(x):
    n, rows = x.shape[:2]
    block = pl.BlockSpec((n, rows // SCAN_STEPS, LANES), lambda g: (0, g, 0))
    return pl.pallas_call(
        scan_kernel, grid=(SCAN_STEPS,), in_specs=[block], out_specs=block,
        out_shape=shape(*x.shape, dtype=WIRE), compiler_params=PARAMS, name="scan",
    )(x)


def scan_back(x):
    n, rows = x.shape[:2]
    return pl.pallas_call(
        scan_back_kernel,
        out_shape=(shape(n, rows - TOLD, LANES, dtype=WIRE), shape(TOLD, LANES)),
        compiler_params=PARAMS,
        name="scan_back",
    )(x)


def exchange(x, axis):
    return lax.all_to_all(x, axis, 0, 0, tiled=True)


def from_behind(block, axis, distance):
    devices = range(lax.axis_size(axis))
    route = [(i - distance, i) for i in devices if i - distance in devices]
    return lax.ppermute(block, axis, route)


def total_over(x, axis):
    n = lax.axis_size(axis)
    bit = 1
    while bit < n:
        masks = [bit] if 2 * bit == n else [bit, 2 * bit, 3 * bit]
        x = x + sum(lax.ppermute(x, axis, [(i, i ^ m) for i in range(n)]) for m in masks)
        bit *= 4
    return x


def body(queries, keys, values, cotangent, conv_weight):
    clips, toks, width = queries.shape
    q, k, v, cot = (x.reshape(toks, width).T for x in (queries, keys, values, cotangent))
    weight = conv_weight.T
    n = lax.axis_size("seq")
    chunk = -(-HALF_ROWS // (PIECE * (n // 2))) * PIECE
    state = shape(chunk * n, LANES)
    sent = shape(*state.shape, dtype=WIRE)
    tokens = shape(width, toks, dtype=bf16)

    half_tokens = shape(width, FRAME, dtype=bf16)

    behind = from_behind(q[:, FRAME:], "seq", 1)
    ahead = from_behind(cot[:, :FRAME], "seq", -1)
    tot, first, send = call(state_kernel, "states", [state, state, sent], k, v)
    got = exchange(send.reshape(n, chunk, LANES), "seq")
    prev = exchange(scan(got), "seq").reshape(state.shape)
    ahead2, prev = lax.optimization_barrier((cot[:, FRAME:], prev))
    ahead2 = from_behind(ahead2, "seq", -1)
    send, conv = shape(n * (chunk + TOLD), LANES, dtype=WIRE), shape(TOLD, LANES)
    att0, att1, att_behind, gtot, glast, send, _ = call(
        functools.partial(middle_kernel, chunk), "middle",
        [half_tokens, half_tokens, half_tokens, state, state, send, conv],
        q, behind, cot, ahead, weight, prev, tot, first, whole=[send, conv],
    )
    got = exchange(send.reshape(n, chunk + TOLD, LANES), "seq")
    att_behind2 = from_behind(att0, "seq", 1)
    follow, conv = scan_back(got)
    follow = exchange(follow, "seq").reshape(state.shape)
    (gq,) = call(
        queries_kernel, "queries", [tokens], q, cot, ahead, ahead2, weight, prev, tot, first
    )
    (mixed,) = call(
        mixed_kernel, "mixed", [tokens], att0, att1, att_behind, att_behind2, weight
    )
    conv = total_over(lax.optimization_barrier((conv, mixed))[0], "dp")
    conv = conv[: 2 * HEADS].reshape(2, HEADS, LANES)[:, :, :HEAD_DIM].reshape(2, width)
    conv = conv / (clips * lax.axis_size("dp"))
    gk, gv = call(last_kernel, "last", [tokens] * 2, k, v, follow, gtot, glast)
    return tuple(x.T.reshape(clips, toks, width) for x in (mixed, gq, gk, gv)) + (conv,)


def solution(mesh):
    blocks = P("dp", "seq", None)
    return jax.shard_map(
        body,
        mesh=mesh,
        in_specs=(blocks,) * 4 + (P(),),
        out_specs=(blocks,) * 4 + (P(),),
        check_vma=False,
    )
```

time: 479 us -> 125 us (0.26); the launches traced: 470 us -> 124 us
  other arithmetic: 165 us -> 0.03 us
  blocking collectives: 127 us -> 0 us
  local copies, waits for them, and re-layouts: 55.3 us -> 9.41 us
  waiting for transfers between devices: 79.1 us -> 33.8 us
  starting transfers between devices: 7.86 us -> 47 us
  Pallas kernels: 0 us -> 32.9 us
  matrix products: 20.2 us -> 0 us
  between operations: 14.7 us -> 0.82 us
    psum x1 -> x0, blocking collectives: 79 us -> none  [body(): lax.psum(local_conv, ('dp', 'seq')) / (clip_count * lax.axis_size('dp'))]
    all_gather x2 -> x0, waiting for transfers between devices: 55.9 us -> none  [entering(): pieces = jax.tree.map(lambda part: lax.all_gather(part, axis), value)]
    all_gather x2 -> x0, blocking collectives: 48.5 us -> none  [entering(): pieces = jax.tree.map(lambda part: lax.all_gather(part, axis), value)]
    select_n x60 -> x0, other arithmetic: 48.1 us -> none  [step(): jnp.where(position < mine, new, old)]
    max x2 -> x0, other arithmetic: 36.5 us -> none  [the longest x1 18.7 us: body(): q_feat = jnp.maximum(queries, 0).reshape(frame_shape)]
    pallas_call x0 -> x7, Pallas kernels: none -> 32.9 us  [the longest x5 27.3 us: call(): pl.pallas_call(kernel, grid=(2,), in_specs=[spec(a) for a in args], out_s...]
    convert_element_type x3 -> x0, other arithmetic: 30.3 us -> none  [the longest x1 14.1 us: body(): jnp.where(queries > 0, grad_q.reshape(out_shape), 0.0).astype(jnp.bfloat16)]
    reduce_sum x5 -> x0, other arithmetic: 27.8 us -> none  [the longest x1 16.8 us: body(): own_keys = jnp.sum(frame_keys, axis=1)]
  transfers between devices with their start and end apart: 4 -> 14, of which waited for: 2 -> 3; matrix products, arithmetic and copies ran while one was open for 29% -> 2% of each run, Pallas kernels for 0% -> 16%
where the time goes in v2:
time: 125 us; the launch traced here: 124 us
  starting transfers between devices  47 us (38%)
  waiting for transfers between devices  33.8 us (27%)
  Pallas kernels  32.9 us (26%)
  local copies, waits for them, and re-layouts  9.41 us (8%)
    pallas_call x5, Pallas kernels, call(): pl.pallas_call(kernel, grid=(2,), in_specs=[spec(a) for a in args], out_s...  27.3 us
    all_to_all x4, starting transfers between devices, exchange(): return lax.all_to_all(x, axis, 0, 0, tiled=True)  25 us
    all_to_all x4, waiting for transfers between devices, exchange(): return lax.all_to_all(x, axis, 0, 0, tiled=True)  19.5 us
    ppermute x4, waiting for transfers between devices, from_behind(): return lax.ppermute(block, axis, route)  14.2 us
    ppermute x4, starting transfers between devices, from_behind(): return lax.ppermute(block, axis, route)  11.3 us
    ppermute x6, starting transfers between devices, total_over(): lax.ppermute(x, axis, [(i, i ^ m) for i in range(n)])  10.7 us
    unnamed x25, local copies, waits for them, and re-layouts  6.72 us
    pallas_call x1, Pallas kernels, scan(): pl.pallas_call(scan_kernel, grid=(SCAN_STEPS,), in_specs=[block], out_spe...  3.14 us
  transfers between devices with their start and end apart: 14, of which 3 were waited for; matrix products, arithmetic and copies ran while one was open for 2% of the time, Pallas kernels for 16%

profile of v2, /device:TPU:2, one launch (start us, length us, event | category | flops | bytes accessed | tf_op | source)
XLA Modules:
  0.0 123.9 jit_solution(17685400812990250708)
XLA Ops:
  0.6 1.9 %slice.20 = bf16[2240,128]{1,0:T(8,128)(2,1)} slice(bf16[2240,256]{1,0:T(8,128)(2,1)} %bitcast.35), slice={[0:2240], [128:256]} | slice | bytes 1146880 | tf_op jit(solution)/shard_map/slice | solution.py:337
  2.5 3.4 %collective-permute-start = (bf16[2240,128]{1,0:T(8,128)(2,1)}, bf16[2240,128]{1,0:T(8,128)(2,1)S(1)}, u32[]{:S(2)}, u32[]{:S(2)}) collective-permute-start(bf16[2240,128]{1,0:T(8,128)(2,1)} %slice.20), channel_id=1, source_target_pairs={{0,1},{1,2},{2,3},{3,4},{4,5},{5,6},{6,7},{7,8},{8,9},{9,10},{10,1... | collective-permute-start | bytes 1720328 | tf_op jit(solution)/shard_map/ppermute | solution.py:312
  5.9 3.7 %states.1 = (f32[2304,128]{1,0:T(8,128)}, f32[2304,128]{1,0:T(8,128)}, bf16[2304,128]{1,0:T(8,128)(2,1)}) custom-call(bf16[2240,256]{1,0:T(8,128)(2,1)} %bitcast.40, bf16[2240,256]{1,0:T(8,128)(2,1)} %bitcast.42), custom_call_target="tpu_custom_call" | custom-call | tf_op jit(solution)/shard_map/states/pallas_call | solution.py:275
  9.7 0.0 copy-start
  9.7 7.3 %all-to-all-start = ((bf16[16,144,128]{2,1,0:T(8,128)(2,1)}), bf16[16,144,128]{2,1,0:T(8,128)(2,1)S(1)}, u32[]{:S(2)}, u32[]{:S(2)}) async-start(bf16[16,144,128]{2,1,0:T(8,128)(2,1)} %bitcast.48), calls=%async_computation | async-start | bytes 1179648 | tf_op jit(solution)/shard_map/all_to_all | solution.py:306
  17.0 0.0 copy-done
  17.0 0.1 fusion
  17.1 0.0 copy-start.11
  17.1 2.0 %collective-permute-start.1 = (bf16[2240,128]{1,0:T(8,128)(2,1)S(1)}, bf16[2240,128]{1,0:T(8,128)(2,1)S(1)}, u32[]{:S(2)}, u32[]{:S(2)}) collective-permute-start(bf16[2240,128]{1,0:T(8,128)(2,1)S(1)} %get-tuple-element.38), channel_id=1, source_target_pairs={{1,0},{2,1},{3,2},{4,3},{5,4},{6,5},{7,6},{8,7},{9,8},{10,9},{11,1... | collective-permute-start | bytes 1720328 | tf_op jit(solution)/shard_map/ppermute | solution.py:312
  19.1 10.2 %all-to-all-done.x_ref = bf16[16,144,128]{2,1,0:T(8,128)(2,1)S(1)} async-done(((bf16[16,144,128]{2,1,0:T(8,128)(2,1)}), bf16[16,144,128]{2,1,0:T(8,128)(2,1)S(1)}, u32[]{:S(2)}, u32[]{:S(2)}) %all-to-all-start) | async-done | bytes 589856 | tf_op jit(solution)/shard_map/all_to_all | solution.py:306
  29.3 0.0 copy-start.4
  29.3 0.8 copy-done.4
  30.1 3.1 %scan.1 = bf16[16,144,128]{2,1,0:T(8,128)(2,1)} custom-call(bf16[16,144,128]{2,1,0:T(8,128)(2,1)} %copy-done.4), custom_call_target="tpu_custom_call" | custom-call | tf_op jit(solution)/shard_map/scan/pallas_call | solution.py:289
  33.2 5.1 %all-to-all-start.1 = ((bf16[16,144,128]{2,1,0:T(8,128)(2,1)}), bf16[16,144,128]{2,1,0:T(8,128)(2,1)S(1)}, u32[]{:S(2)}, u32[]{:S(2)}) async-start(bf16[16,144,128]{2,1,0:T(8,128)(2,1)} %scan.1), calls=%async_computation.1 | async-start | bytes 1179648 | tf_op jit(solution)/shard_map/all_to_all | solution.py:306
  38.4 0.0 copy-done.11
  38.4 1.4 %copy.11 = f32[2,2240]{0,1:T(8,128)} copy(f32[2,2240]{1,0:T(2,128)S(1)} %copy-done.11) | data formatting | bytes 35840 | tf_op args[4]
  39.8 9.4 %all-to-all-done.1 = bf16[16,144,128]{2,1,0:T(8,128)(2,1)S(1)} async-done(((bf16[16,144,128]{2,1,0:T(8,128)(2,1)}), bf16[16,144,128]{2,1,0:T(8,128)(2,1)S(1)}, u32[]{:S(2)}, u32[]{:S(2)}) %all-to-all-start.1) | async-done | bytes 589856 | tf_op jit(solution)/shard_map/all_to_all | solution.py:306
  49.1 0.0 copy-start.1
  49.1 0.0 collective-permute-done.behind_ref
  49.1 0.0 copy-start.7
  49.1 0.0 collective-permute-done.1.ahead_ref
  49.1 0.0 copy-start.5
  49.1 0.8 copy-done.1
  50.0 0.2 copy-done.7
  50.1 0.2 copy-done.5
  50.3 8.1 %middle.1 = (bf16[2240,128]{1,0:T(8,128)(2,1)}, bf16[2240,128]{1,0:T(8,128)(2,1)}, bf16[2240,128]{1,0:T(8,128)(2,1)}, f32[2304,128]{1,0:T(8,128)}, f32[2304,128]...) custom-call(bf16[2240,256]{1,0:T(8,128)(2,1)} %bitcast.36, bf16[2240,128]{1,0:T(8,128)(2,1)} %copy-done.7, ...), custom_call_target="tpu_custom_call" | custom-call | tf_op jit(solution)/shard_map/middle/pallas_call | solution.py:275
  58.4 0.0 copy-start.8
  58.4 5.0 %all-to-all-start.2 = ((bf16[16,192,128]{2,1,0:T(8,128)(2,1)}), bf16[16,192,128]{2,1,0:T(8,128)(2,1)S(1)}, u32[]{:S(2)}, u32[]{:S(2)}) async-start(bf16[16,192,128]{2,1,0:T(8,128)(2,1)} %bitcast.47), calls=%async_computation.2 | async-start | bytes 1572864 | tf_op jit(solution)/shard_map/all_to_all | solution.py:306
  63.4 0.0 copy-done.8
  63.4 3.4 %collective-permute-start.2 = (bf16[2240,128]{1,0:T(8,128)(2,1)S(1)}, bf16[2240,128]{1,0:T(8,128)(2,1)S(1)}, u32[]{:S(2)}, u32[]{:S(2)}) collective-permute-start(bf16[2240,128]{1,0:T(8,128)(2,1)S(1)} %copy-done.8), channel_id=1, source_target_pairs={{0,1},{1,2},{2,3},{3,4},{4,5},{5,6},{6,7},{7,8},{8,9},{9,10},{10,1... | collective-permute-start | bytes 1720328 | tf_op jit(solution)/shard_map/ppermute | solution.py:312
  66.8 2.5 %collective-permute-start.3 = (bf16[2240,128]{1,0:T(8,128)(2,1)S(1)}, bf16[2240,128]{1,0:T(8,128)(2,1)S(1)}, u32[]{:S(2)}, u32[]{:S(2)}) collective-permute-start(bf16[2240,128]{1,0:T(8,128)(2,1)S(1)} %get-tuple-element.28), channel_id=1, source_target_pairs={{1,0},{2,1},{3,2},{4,3},{5,4},{6,5},{7,6},{8,7},{9,8},{10,9},{11,1... | collective-permute-start | bytes 1720328 | tf_op jit(solution)/shard_map/ppermute | solution.py:312
  69.3 14.2 %collective-permute-done.2.behind2_ref = bf16[2240,128]{1,0:T(8,128)(2,1)S(1)} collective-permute-done((bf16[2240,128]{1,0:T(8,128)(2,1)S(1)}, bf16[2240,128]{1,0:T(8,128)(2,1)S(1)}, u32[]{:S(2)}, u32[]{:S(2)}) %collective-permute-start.2) | collective-permute-done | bytes 573472 | tf_op jit(solution)/shard_map/ppermute | solution.py:312
  83.6 0.0 copy-start.9
  83.6 0.8 copy-done.9
  84.4 3.7 %mixed.1 = bf16[2240,256]{1,0:T(8,128)(2,1)} custom-call(bf16[2240,128]{1,0:T(8,128)(2,1)} %get-tuple-element.25.att0_ref, bf16[2240,128]{1,0:T(8,128)(2,1)} %get-tuple-element.26.att1_ref, bf16[2240,128]{1,0:T(8,128)(2,1)} %get-tuple-element.27.behind_ref, bf16[2240,128]{1,0:T(8,128)(2,1)} %copy-done.9, f32[2240,2]{1,0:T(8,128)} %bitcast.30), custom_call_target="tpu_custom_call" | custom-call | tf_op jit(solution)/shard_map/mixed/pallas_call | solution.py:275
  88.1 0.0 all-to-all-done.2.x_ref
  88.1 0.0 copy-start.2
  88.1 0.9 copy-done.2
  88.9 2.4 %scan_back.1 = (bf16[16,144,128]{2,1,0:T(8,128)(2,1)}, f32[48,128]{1,0:T(8,128)}) custom-call(bf16[16,192,128]{2,1,0:T(8,128)(2,1)} %copy-done.2), custom_call_target="tpu_custom_call" | custom-call | tf_op jit(solution)/shard_map/scan_back/pallas_call | solution.py:297
  91.4 0.0 copy-start.10
  91.4 0.0 collective-permute-start.6
  91.4 2.0 %collective-permute-start.5 = (f32[48,128]{1,0:T(8,128)}, f32[48,128]{1,0:T(8,128)S(1)}, u32[]{:S(2)}, u32[]{:S(2)}) collective-permute-start(f32[48,128]{1,0:T(8,128)} %get-tuple-element.36), channel_id=1, source_target_pairs={{0,32},{16,48},{32,0},{48,16},{64,96},{80,112},{96,64},{112,80},{1... | collective-permute-start | bytes 73736 | tf_op jit(solution)/shard_map/ppermute | solution.py:320
  93.3 0.1 collective-permute-start.4
  93.4 7.5 %all-to-all-start.3 = ((bf16[16,144,128]{2,1,0:T(8,128)(2,1)}), bf16[16,144,128]{2,1,0:T(8,128)(2,1)S(1)}, u32[]{:S(2)}, u32[]{:S(2)}) async-start(bf16[16,144,128]{2,1,0:T(8,128)(2,1)} %get-tuple-element.30), calls=%async_computation.3 | async-start | bytes 1179648 | tf_op jit(solution)/shard_map/all_to_all | solution.py:306
  101.0 0.0 collective-permute-done.6
  101.0 0.0 collective-permute-done.5
  101.0 0.0 collective-permute-done.4
  101.0 0.0 copy-done.10
  101.0 6.2 %collective-permute-start.9 = (f32[48,128]{1,0:T(8,128)S(1)}, f32[48,128]{1,0:T(8,128)S(1)}, u32[]{:S(2)}, u32[]{:S(2)}) collective-permute-start(f32[48,128]{1,0:T(8,128)S(1)} %add_add_fusion), channel_id=1, source_target_pairs={{0,192},{16,208},{32,224},{48,240},{64,128},{80,144},{96,160},{112... | collective-permute-start | bytes 73736 | tf_op jit(solution)/shard_map/ppermute | solution.py:320
  107.2 1.0 collective-permute-start.8
  108.2 1.5 %collective-permute-start.7 = (f32[48,128]{1,0:T(8,128)S(1)}, f32[48,128]{1,0:T(8,128)S(1)}, u32[]{:S(2)}, u32[]{:S(2)}) collective-permute-start(f32[48,128]{1,0:T(8,128)S(1)} %add_add_fusion), channel_id=1, source_target_pairs={{0,64},{16,80},{32,96},{48,112},{64,0},{80,16},{96,32},{112,48},{1... | collective-permute-start | bytes 73736 | tf_op jit(solution)/shard_map/ppermute | solution.py:320
  109.7 0.0 collective-permute-done.3.ahead2_ref
  109.7 0.0 copy-start.6
  109.7 0.8 copy-done.6
  110.5 6.7 %queries.1 = bf16[2240,256]{1,0:T(8,128)(2,1)} custom-call(bf16[2240,256]{1,0:T(8,128)(2,1)} %bitcast.37, bf16[2240,256]{1,0:T(8,128)(2,1)} %bitcast.33, bf16[2240,128]{1,0:T(8,128)(2,1)} %copy-done.5, bf16[2240,128]{1,0:T(8,128)(2,1)} %copy-done.6, f32[2240,2]{1,0:T(8,128)} %bitcast.31, bf16[2304,128]{1,0:T(8,128)(2,1)} %bitcast.39, ...), custom_call_target="tpu_custom_call" | custom-call | tf_op jit(solution)/shard_map/queries/pallas_call | solution.py:275
  117.2 0.0 collective-permute-done.9
  117.2 0.0 collective-permute-done.8
  117.2 0.0 collective-permute-done.7
  117.2 0.7 div.10
  117.9 0.0 all-to-all-done.3
  117.9 0.0 copy-start.3
  117.9 0.8 copy-done.3
  118.8 5.2 %last.1 = (bf16[2240,256]{1,0:T(8,128)(2,1)}, bf16[2240,256]{1,0:T(8,128)(2,1)}) custom-call(bf16[2240,256]{1,0:T(8,128)(2,1)} %bitcast.41, bf16[2240,256]{1,0:T(8,128)(2,1)} %bitcast.43, bf16[2304,128]{1,0:T(8,128)(2,1)} %bitcast.44, f32[2304,128]{1,0:T(8,128)} %get-tuple-element.31.gtot_ref, f32[2304,128]{1,0:T(8,128)} %get-tuple-element.32.glast_ref), custom_call_target="tpu_custom_call" | custom-call | tf_op jit(solution)/shard_map/last/pallas_call | solution.py:275
  (4 shorter events, 0.0 us)
Async XLA Ops:
  2.5 46.6 %collective-permute-start = (bf16[2240,128]{1,0:T(8,128)(2,1)}, bf16[2240,128]{1,0:T(8,128)(2,1)S(1)}, u32[]{:S(2)}, u32[]{:S(2)}) collective-permute-start(bf16[2240,128]{1,0:T(8,128)(2,1)} %slice.20), channel_id=1, source_target_pairs={{0,1},{1,2},{2,3},{3,4},{4,5},{5,6},{6,7},{7,8},{8,9},{9,10},{10,1... | collective-permute-start | bytes 1720328 | tf_op jit(solution)/shard_map/ppermute | solution.py:312
  9.7 7.3 %copy-start = (bf16[1,256,2240]{1,2,0:T(8,128)(2,1)S(1)}, bf16[1,256,2240]{1,2,0:T(8,128)(2,1)}, u32[]{:S(2)}) copy-start(bf16[1,256,2240]{1,2,0:T(8,128)(2,1)} %param.8) | copy-start | bytes 3440644
  9.7 19.6 %all-to-all-start = ((bf16[16,144,128]{2,1,0:T(8,128)(2,1)}), bf16[16,144,128]{2,1,0:T(8,128)(2,1)S(1)}, u32[]{:S(2)}, u32[]{:S(2)}) async-start(bf16[16,144,128]{2,1,0:T(8,128)(2,1)} %bitcast.48), calls=%async_computation | async-start | bytes 1179648 | tf_op jit(solution)/shard_map/all_to_all | solution.py:306
  17.1 21.3 %copy-start.11 = (f32[2,2240]{1,0:T(2,128)S(1)}, f32[2,2240]{1,0:T(2,128)}, u32[]{:S(2)}) copy-start(f32[2,2240]{1,0:T(2,128)} %param.9) | copy-start | bytes 53764
  17.1 32.1 %collective-permute-start.1 = (bf16[2240,128]{1,0:T(8,128)(2,1)S(1)}, bf16[2240,128]{1,0:T(8,128)(2,1)S(1)}, u32[]{:S(2)}, u32[]{:S(2)}) collective-permute-start(bf16[2240,128]{1,0:T(8,128)(2,1)S(1)} %get-tuple-element.38), channel_id=1, source_target_pairs={{1,0},{2,1},{3,2},{4,3},{5,4},{6,5},{7,6},{8,7},{9,8},{10,9},{11,1... | collective-permute-start | bytes 1720328 | tf_op jit(solution)/shard_map/ppermute | solution.py:312
  29.3 0.8 copy-start.4
  33.2 15.9 %all-to-all-start.1 = ((bf16[16,144,128]{2,1,0:T(8,128)(2,1)}), bf16[16,144,128]{2,1,0:T(8,128)(2,1)S(1)}, u32[]{:S(2)}, u32[]{:S(2)}) async-start(bf16[16,144,128]{2,1,0:T(8,128)(2,1)} %scan.1), calls=%async_computation.1 | async-start | bytes 1179648 | tf_op jit(solution)/shard_map/all_to_all | solution.py:306
  49.1 0.8 copy-start.1
  49.1 1.0 copy-start.7
  49.1 1.2 copy-start.5
  58.4 5.0 %copy-start.8 = (bf16[2240,128]{1,0:T(8,128)(2,1)S(1)}, bf16[2240,128]{1,0:T(8,128)(2,1)}, u32[]{:S(2)}) copy-start(bf16[2240,128]{1,0:T(8,128)(2,1)} %get-tuple-element.25.att0_ref) | copy-start | bytes 1720324
  58.4 29.6 %all-to-all-start.2 = ((bf16[16,192,128]{2,1,0:T(8,128)(2,1)}), bf16[16,192,128]{2,1,0:T(8,128)(2,1)S(1)}, u32[]{:S(2)}, u32[]{:S(2)}) async-start(bf16[16,192,128]{2,1,0:T(8,128)(2,1)} %bitcast.47), calls=%async_computation.2 | async-start | bytes 1572864 | tf_op jit(solution)/shard_map/all_to_all | solution.py:306
  63.4 20.1 %collective-permute-start.2 = (bf16[2240,128]{1,0:T(8,128)(2,1)S(1)}, bf16[2240,128]{1,0:T(8,128)(2,1)S(1)}, u32[]{:S(2)}, u32[]{:S(2)}) collective-permute-start(bf16[2240,128]{1,0:T(8,128)(2,1)S(1)} %copy-done.8), channel_id=1, source_target_pairs={{0,1},{1,2},{2,3},{3,4},{4,5},{5,6},{6,7},{7,8},{8,9},{9,10},{10,1... | collective-permute-start | bytes 1720328 | tf_op jit(solution)/shard_map/ppermute | solution.py:312
  66.8 42.9 %collective-permute-start.3 = (bf16[2240,128]{1,0:T(8,128)(2,1)S(1)}, bf16[2240,128]{1,0:T(8,128)(2,1)S(1)}, u32[]{:S(2)}, u32[]{:S(2)}) collective-permute-start(bf16[2240,128]{1,0:T(8,128)(2,1)S(1)} %get-tuple-element.28), channel_id=1, source_target_pairs={{1,0},{2,1},{3,2},{4,3},{5,4},{6,5},{7,6},{8,7},{9,8},{10,9},{11,1... | collective-permute-start | bytes 1720328 | tf_op jit(solution)/shard_map/ppermute | solution.py:312
  83.6 0.8 copy-start.9
  88.1 0.9 copy-start.2
  91.4 9.6 %copy-start.10 = (f32[48,128]{1,0:T(8,128)S(1)}, f32[48,128]{1,0:T(8,128)}, u32[]{:S(2)}) copy-start(f32[48,128]{1,0:T(8,128)} %get-tuple-element.36) | copy-start | bytes 73732
  91.4 9.6 %collective-permute-start.6 = (f32[48,128]{1,0:T(8,128)}, f32[48,128]{1,0:T(8,128)S(1)}, u32[]{:S(2)}, u32[]{:S(2)}) collective-permute-start(f32[48,128]{1,0:T(8,128)} %get-tuple-element.36), channel_id=1, source_target_pairs={{0,48},{16,32},{32,16},{48,0},{64,112},{80,96},{96,80},{112,64},{1... | collective-permute-start | bytes 73736 | tf_op jit(solution)/shard_map/ppermute | solution.py:320
  91.4 9.6 %collective-permute-start.5 = (f32[48,128]{1,0:T(8,128)}, f32[48,128]{1,0:T(8,128)S(1)}, u32[]{:S(2)}, u32[]{:S(2)}) collective-permute-start(f32[48,128]{1,0:T(8,128)} %get-tuple-element.36), channel_id=1, source_target_pairs={{0,32},{16,48},{32,0},{48,16},{64,96},{80,112},{96,64},{112,80},{1... | collective-permute-start | bytes 73736 | tf_op jit(solution)/shard_map/ppermute | solution.py:320
  93.3 7.6 %collective-permute-start.4 = (f32[48,128]{1,0:T(8,128)}, f32[48,128]{1,0:T(8,128)S(1)}, u32[]{:S(2)}, u32[]{:S(2)}) collective-permute-start(f32[48,128]{1,0:T(8,128)} %get-tuple-element.36), channel_id=1, source_target_pairs={{0,16},{16,0},{32,48},{48,32},{64,80},{80,64},{96,112},{112,96},{1... | collective-permute-start | bytes 73736 | tf_op jit(solution)/shard_map/ppermute | solution.py:320
  93.4 24.5 %all-to-all-start.3 = ((bf16[16,144,128]{2,1,0:T(8,128)(2,1)}), bf16[16,144,128]{2,1,0:T(8,128)(2,1)S(1)}, u32[]{:S(2)}, u32[]{:S(2)}) async-start(bf16[16,144,128]{2,1,0:T(8,128)(2,1)} %get-tuple-element.30), calls=%async_computation.3 | async-start | bytes 1179648 | tf_op jit(solution)/shard_map/all_to_all | solution.py:306
  101.0 16.2 %collective-permute-start.9 = (f32[48,128]{1,0:T(8,128)S(1)}, f32[48,128]{1,0:T(8,128)S(1)}, u32[]{:S(2)}, u32[]{:S(2)}) collective-permute-start(f32[48,128]{1,0:T(8,128)S(1)} %add_add_fusion), channel_id=1, source_target_pairs={{0,192},{16,208},{32,224},{48,240},{64,128},{80,144},{96,160},{112... | collective-permute-start | bytes 73736 | tf_op jit(solution)/shard_map/ppermute | solution.py:320
  107.2 9.9 %collective-permute-start.8 = (f32[48,128]{1,0:T(8,128)S(1)}, f32[48,128]{1,0:T(8,128)S(1)}, u32[]{:S(2)}, u32[]{:S(2)}) collective-permute-start(f32[48,128]{1,0:T(8,128)S(1)} %add_add_fusion), channel_id=1, source_target_pairs={{0,128},{16,144},{32,160},{48,176},{64,192},{80,208},{96,224},{112... | collective-permute-start | bytes 73736 | tf_op jit(solution)/shard_map/ppermute | solution.py:320
  108.2 9.0 %collective-permute-start.7 = (f32[48,128]{1,0:T(8,128)S(1)}, f32[48,128]{1,0:T(8,128)S(1)}, u32[]{:S(2)}, u32[]{:S(2)}) collective-permute-start(f32[48,128]{1,0:T(8,128)S(1)} %add_add_fusion), channel_id=1, source_target_pairs={{0,64},{16,80},{32,96},{48,112},{64,0},{80,16},{96,32},{112,48},{1... | collective-permute-start | bytes 73736 | tf_op jit(solution)/shard_map/ppermute | solution.py:320
  109.7 0.8 copy-start.6
  117.9 0.8 copy-start.3

commit v3 on v2

--- a/solution.py
+++ b/solution.py
@@ -16,7 +16,6 @@
 PIECE = 16
 TOLD = 48
 WIRE = jnp.bfloat16
-SCAN_STEPS = 1
 
 denom_eps = 1e-06
 loss_scale = 16.0
@@ -139,15 +138,16 @@
         o_ref[i] = total
 
 
-def scan_back_kernel(x_ref, o_ref, sum_ref):
-    n, rows = o_ref.shape[:2]
-    parts = [decode_grad(x_ref[i, :rows]) for i in range(n)]
+def scan_back_kernel(x_ref, conv_ref, o_ref):
+    n, rows = x_ref.shape[:2]
+    conv = conv_ref[...].astype(WIRE)
+    parts = [decode_grad(x_ref[i]) for i in range(n)]
     totals = [jnp.zeros_like(parts[0])]
     for part in parts[:0:-1]:
         totals.append(totals[-1] + part)
     for i, total in enumerate([encode_grad(total) for total in totals]):
-        o_ref[n - 1 - i] = total
-    sum_ref[...] = sum(x_ref[i, rows:].astype(f32) for i in range(n))
+        o_ref[n - 1 - i, :rows] = total
+        o_ref[n - 1 - i, rows:] = conv
 
 
 def numerators(qs, states):
@@ -163,11 +163,10 @@
 
 
 def middle_kernel(
-    chunk, q_ref, behind_ref, cot_ref, ahead_ref, w_ref, prev_ref, tot_ref, first_ref,
+    q_ref, behind_ref, cot_ref, ahead_ref, w_ref, prev_ref, tot_ref, first_ref,
     att0_ref, att1_ref, att_behind_ref, gtot_ref, glast_ref, send_ref, conv_ref,
 ):
     step = pl.program_id(0)
-    stride = chunk + TOLD
     qs, states, cots, gos = {}, {}, {}, {}
     for j in range(HALF):
         rows = rows_of(j)
@@ -194,11 +193,7 @@
         own = gstates[j, 0] + gstates[j, 1]
         glast_ref[rows, :] = gstates[j, 1]
         gtot_ref[rows, :] = own
-        wire = encode_grad(own + gstates[j, -1])
-        for at in range(rows.start, rows.stop, PIECE):
-            to = step * (send_ref.shape[0] // 2) + at // chunk * stride + at % chunk
-            piece = wire[at - rows.start : at - rows.start + PIECE]
-            send_ref[pl.ds(pl.multiple_of(to, PIECE), PIECE), :] = piece
+        send_ref[rows, :] = encode_grad(own + gstates[j, -1])
         att_behind_ref[rows, :], att0_ref[rows, :], att1_ref[rows, :] = (
             atts[j, f] for f in (-1, 0, 1)
         )
@@ -212,9 +207,6 @@
     @pl.when(step == 1)
     def _():
         conv_ref[2 * HEADS :, :] = jnp.zeros((TOLD - 2 * HEADS, LANES), f32)
-        conv = conv_ref[...].astype(send_ref.dtype)
-        for i in range(send_ref.shape[0] // stride):
-            send_ref[i * stride + chunk : (i + 1) * stride, :] = conv
 
 
 def queries_kernel(
@@ -247,13 +239,29 @@
             mix_ref[rows, frames[f]] = filtered(c[f : f + 3][::-1], w_ref, rows).astype(bf16)
 
 
-def last_kernel(k_ref, v_ref, follow_ref, gtot_ref, glast_ref, gk_ref, gv_ref):
+def last_kernel(chunk, k_ref, v_ref, follow_ref, gtot_ref, glast_ref, gk_ref, gv_ref, conv_ref):
+    stride = chunk + TOLD
+    starts = range(0, follow_ref.shape[0], stride)
+    conv = sum(follow_ref[i + chunk : i + stride, :].astype(f32) for i in starts)
+
+    @pl.when(pl.program_id(0) == 0)
+    def _():
+        conv_ref[...] = conv
+
+    @pl.when(pl.program_id(0) > 0)
+    def _():
+        conv_ref[...] += conv
+
     ks, vs, states = {}, {}, {}
     for j in range(HALF):
         rows = rows_of(j)
         k = jnp.maximum(k_ref[rows, :], 0)
         v = with_one(v_ref[rows, :])
-        behind = decode_grad(follow_ref[rows, :])
+        pieces = []
+        for at in range(rows.start, rows.stop, PIECE):
+            place = at // chunk * stride + at % chunk
+            pieces.append(follow_ref[place : place + PIECE, :])
+        behind = decode_grad(cat(pieces, 0))
         for f in range(2):
             ks[j, f], vs[j, f] = k[:, frames[f]], v[:, frames[f]]
             states[j, f] = split(behind + (gtot_ref, glast_ref)[f][rows, :])
@@ -283,23 +291,15 @@
     )(*args)
 
 
-def scan(x):
+def scan(kernel, name, x, told=None):
     n, rows = x.shape[:2]
-    block = pl.BlockSpec((n, rows // SCAN_STEPS, LANES), lambda g: (0, g, 0))
+    args = (x,) if told is None else (x, told)
     return pl.pallas_call(
-        scan_kernel, grid=(SCAN_STEPS,), in_specs=[block], out_specs=block,
-        out_shape=shape(*x.shape, dtype=WIRE), compiler_params=PARAMS, name="scan",
-    )(x)
-
-
-def scan_back(x):
-    n, rows = x.shape[:2]
-    return pl.pallas_call(
-        scan_back_kernel,
-        out_shape=(shape(n, rows - TOLD, LANES, dtype=WIRE), shape(TOLD, LANES)),
+        kernel,
+        out_shape=shape(n, rows + sum(a.shape[0] for a in args[1:]), LANES, dtype=WIRE),
         compiler_params=PARAMS,
-        name="scan_back",
-    )(x)
+        name=name,
+    )(*args)
 
 
 def exchange(x, axis):
@@ -338,29 +338,36 @@
     ahead = from_behind(cot[:, :FRAME], "seq", -1)
     tot, first, send = call(state_kernel, "states", [state, state, sent], k, v)
     got = exchange(send.reshape(n, chunk, LANES), "seq")
-    prev = exchange(scan(got), "seq").reshape(state.shape)
+    prev = exchange(scan(scan_kernel, "scan", got), "seq").reshape(state.shape)
     ahead2, prev = lax.optimization_barrier((cot[:, FRAME:], prev))
     ahead2 = from_behind(ahead2, "seq", -1)
-    send, conv = shape(n * (chunk + TOLD), LANES, dtype=WIRE), shape(TOLD, LANES)
-    att0, att1, att_behind, gtot, glast, send, _ = call(
-        functools.partial(middle_kernel, chunk), "middle",
-        [half_tokens, half_tokens, half_tokens, state, state, send, conv],
-        q, behind, cot, ahead, weight, prev, tot, first, whole=[send, conv],
-    )
-    got = exchange(send.reshape(n, chunk + TOLD, LANES), "seq")
+    conv = shape(TOLD, LANES)
+    att0, att1, att_behind, gtot, glast, send, conv = call(
+        middle_kernel, "middle",
+        [half_tokens, half_tokens, half_tokens, state, state, sent, conv],
+        q, behind, cot, ahead, weight, prev, tot, first, whole=[conv],
+    )
+    conv = total_over(conv, "dp")
+    got = exchange(send.reshape(n, chunk, LANES), "seq")
     att_behind2 = from_behind(att0, "seq", 1)
-    follow, conv = scan_back(got)
-    follow = exchange(follow, "seq").reshape(state.shape)
+    follow = scan(scan_back_kernel, "scan_back", got, conv)
+    att_behind2 = lax.optimization_barrier((att_behind2, follow))[0]
+    ahead2 = lax.optimization_barrier((ahead2, follow))[0]
+    follow, att_behind2, ahead2 = lax.optimization_barrier((follow, att_behind2, ahead2))
+    follow = exchange(follow, "seq").reshape(-1, LANES)
     (gq,) = call(
         queries_kernel, "queries", [tokens], q, cot, ahead, ahead2, weight, prev, tot, first
     )
     (mixed,) = call(
         mixed_kernel, "mixed", [tokens], att0, att1, att_behind, att_behind2, weight
     )
-    conv = total_over(lax.optimization_barrier((conv, mixed))[0], "dp")
+    conv = shape(TOLD, LANES)
+    gk, gv, conv = call(
+        functools.partial(last_kernel, chunk), "last", [tokens, tokens, conv],
+        k, v, follow, gtot, glast, whole=[conv],
+    )
     conv = conv[: 2 * HEADS].reshape(2, HEADS, LANES)[:, :, :HEAD_DIM].reshape(2, width)
     conv = conv / (clips * lax.axis_size("dp"))
-    gk, gv = call(last_kernel, "last", [tokens] * 2, k, v, follow, gtot, glast)
     return tuple(x.T.reshape(clips, toks, width) for x in (mixed, gq, gk, gv)) + (conv,)
 
 

time: 125 us -> 120 us (0.960)
  waiting for transfers between devices: 33.8 us -> 28.5 us
  starting transfers between devices: 47 us -> 48.4 us
    ppermute x4, waiting for transfers between devices: 14.2 us -> 0.01 us  [from_behind(): return lax.ppermute(block, axis, route)]
    ppermute x6, waiting for transfers between devices: 0.02 us -> 7.45 us  [total_over(): lax.ppermute(x, axis, [(i, i ^ m) for i in range(n)])]
    unnamed x25 -> x23, local copies, waits for them, and re-layouts: 6.72 us -> 4.93 us
    all_to_all x4, waiting for transfers between devices: 19.5 us -> 21.1 us  [exchange(): return lax.all_to_all(x, axis, 0, 0, tiled=True)]
  transfers between devices with their start and end apart: 14 -> 14, of which waited for: 3 -> 6; matrix products, arithmetic and copies ran while one was open for 2% -> 2% of each run, Pallas kernels for 16% -> 23%
where the time goes in v3:
time: 120 us
  starting transfers between devices  48.4 us (40%)
  Pallas kernels  32.9 us (27%)
  waiting for transfers between devices  28.5 us (24%)
  local copies, waits for them, and re-layouts  8.35 us (7%)
    pallas_call x5, Pallas kernels, call(): pl.pallas_call(kernel, grid=(2,), in_specs=[spec(a) for a in args], out_s...  27.3 us
    all_to_all x4, starting transfers between devices, exchange(): return lax.all_to_all(x, axis, 0, 0, tiled=True)  26 us
    all_to_all x4, waiting for transfers between devices, exchange(): return lax.all_to_all(x, axis, 0, 0, tiled=True)  21.1 us
    ppermute x4, starting transfers between devices, from_behind(): return lax.ppermute(block, axis, route)  11.2 us
    ppermute x6, starting transfers between devices, total_over(): lax.ppermute(x, axis, [(i, i ^ m) for i in range(n)])  11.1 us
    ppermute x6, waiting for transfers between devices, total_over(): lax.ppermute(x, axis, [(i, i ^ m) for i in range(n)])  7.45 us
    pallas_call x2, Pallas kernels, scan(): pl.pallas_call(kernel, out_shape=shape(n, rows + sum((a.shape[0] for a in...  5.57 us
    unnamed x23, local copies, waits for them, and re-layouts  4.93 us
  transfers between devices with their start and end apart: 14, of which 6 were waited for; matrix products, arithmetic and copies ran while one was open for 2% of the time, Pallas kernels for 23%

profile of v3, /device:TPU:2, one launch (start us, length us, event | category | flops | bytes accessed | tf_op | source)
XLA Modules:
  0.0 119.5 jit_solution(1573294887798228098)
XLA Ops:
  0.6 1.9 %slice.20 = bf16[2240,128]{1,0:T(8,128)(2,1)} slice(bf16[2240,256]{1,0:T(8,128)(2,1)} %bitcast.35), slice={[0:2240], [128:256]} | slice | bytes 1146880 | tf_op jit(solution)/shard_map/slice | solution.py:337
  2.5 3.4 %collective-permute-start = (bf16[2240,128]{1,0:T(8,128)(2,1)}, bf16[2240,128]{1,0:T(8,128)(2,1)S(1)}, u32[]{:S(2)}, u32[]{:S(2)}) collective-permute-start(bf16[2240,128]{1,0:T(8,128)(2,1)} %slice.20), channel_id=1, source_target_pairs={{0,1},{1,2},{2,3},{3,4},{4,5},{5,6},{6,7},{7,8},{8,9},{9,10},{10,1... | collective-permute-start | bytes 1720328 | tf_op jit(solution)/shard_map/ppermute | solution.py:312
  5.9 3.7 %states.1 = (f32[2304,128]{1,0:T(8,128)}, f32[2304,128]{1,0:T(8,128)}, bf16[2304,128]{1,0:T(8,128)(2,1)}) custom-call(bf16[2240,256]{1,0:T(8,128)(2,1)} %bitcast.40, bf16[2240,256]{1,0:T(8,128)(2,1)} %bitcast.42), custom_call_target="tpu_custom_call" | custom-call | tf_op jit(solution)/shard_map/states/pallas_call | solution.py:283
  9.7 0.0 copy-start
  9.7 7.3 %all-to-all-start = ((bf16[16,144,128]{2,1,0:T(8,128)(2,1)}), bf16[16,144,128]{2,1,0:T(8,128)(2,1)S(1)}, u32[]{:S(2)}, u32[]{:S(2)}) async-start(bf16[16,144,128]{2,1,0:T(8,128)(2,1)} %bitcast.48), calls=%async_computation | async-start | bytes 1179648 | tf_op jit(solution)/shard_map/all_to_all | solution.py:306
  17.0 0.0 copy-done
  17.0 0.1 fusion
  17.1 0.0 copy-start.10
  17.1 2.0 %collective-permute-start.1 = (bf16[2240,128]{1,0:T(8,128)(2,1)S(1)}, bf16[2240,128]{1,0:T(8,128)(2,1)S(1)}, u32[]{:S(2)}, u32[]{:S(2)}) collective-permute-start(bf16[2240,128]{1,0:T(8,128)(2,1)S(1)} %get-tuple-element.46), channel_id=1, source_target_pairs={{1,0},{2,1},{3,2},{4,3},{5,4},{6,5},{7,6},{8,7},{9,8},{10,9},{11,1... | collective-permute-start | bytes 1720328 | tf_op jit(solution)/shard_map/ppermute | solution.py:312
  19.1 10.2 %all-to-all-done.x_ref = bf16[16,144,128]{2,1,0:T(8,128)(2,1)S(1)} async-done(((bf16[16,144,128]{2,1,0:T(8,128)(2,1)}), bf16[16,144,128]{2,1,0:T(8,128)(2,1)S(1)}, u32[]{:S(2)}, u32[]{:S(2)}) %all-to-all-start) | async-done | bytes 589856 | tf_op jit(solution)/shard_map/all_to_all | solution.py:306
  29.3 0.0 copy-start.3
  29.3 0.8 copy-done.3
  30.1 3.1 %scan.1 = bf16[16,144,128]{2,1,0:T(8,128)(2,1)} custom-call(bf16[16,144,128]{2,1,0:T(8,128)(2,1)} %copy-done.3), custom_call_target="tpu_custom_call" | custom-call | tf_op jit(solution)/shard_map/scan/pallas_call | solution.py:297
  33.2 5.1 %all-to-all-start.1 = ((bf16[16,144,128]{2,1,0:T(8,128)(2,1)}), bf16[16,144,128]{2,1,0:T(8,128)(2,1)S(1)}, u32[]{:S(2)}, u32[]{:S(2)}) async-start(bf16[16,144,128]{2,1,0:T(8,128)(2,1)} %scan.1), calls=%async_computation.1 | async-start | bytes 1179648 | tf_op jit(solution)/shard_map/all_to_all | solution.py:306
  38.4 0.0 copy-done.10
  38.4 1.4 %copy.11 = f32[2,2240]{0,1:T(8,128)} copy(f32[2,2240]{1,0:T(2,128)S(1)} %copy-done.10) | data formatting | bytes 35840 | tf_op args[4]
  39.8 9.4 %all-to-all-done.1 = bf16[16,144,128]{2,1,0:T(8,128)(2,1)S(1)} async-done(((bf16[16,144,128]{2,1,0:T(8,128)(2,1)}), bf16[16,144,128]{2,1,0:T(8,128)(2,1)S(1)}, u32[]{:S(2)}, u32[]{:S(2)}) %all-to-all-start.1) | async-done | bytes 589856 | tf_op jit(solution)/shard_map/all_to_all | solution.py:306
  49.1 0.0 copy-start.1
  49.1 3.4 %collective-permute-start.9 = (bf16[2240,128]{1,0:T(8,128)(2,1)S(1)}, bf16[2240,128]{1,0:T(8,128)(2,1)S(1)}, u32[]{:S(2)}, u32[]{:S(2)}) collective-permute-start(bf16[2240,128]{1,0:T(8,128)(2,1)S(1)} %get-tuple-element.35), channel_id=1, source_target_pairs={{1,0},{2,1},{3,2},{4,3},{5,4},{6,5},{7,6},{8,7},{9,8},{10,9},{11,1... | collective-permute-start | bytes 1720328 | tf_op jit(solution)/shard_map/ppermute | solution.py:312
  52.5 0.0 collective-permute-done.behind_ref
  52.5 0.0 copy-start.8
  52.5 0.0 collective-permute-done.1.ahead_ref
  52.5 0.0 copy-start.5
  52.5 0.0 copy-done.1
  52.5 0.8 copy-done.8
  53.3 0.2 copy-done.5
  53.5 7.9 %middle.1 = (bf16[2240,128]{1,0:T(8,128)(2,1)}, bf16[2240,128]{1,0:T(8,128)(2,1)}, bf16[2240,128]{1,0:T(8,128)(2,1)}, f32[2304,128]{1,0:T(8,128)}, f32[2304,128]...) custom-call(bf16[2240,256]{1,0:T(8,128)(2,1)} %bitcast.36, bf16[2240,128]{1,0:T(8,128)(2,1)} %copy-done.8, ...), custom_call_target="tpu_custom_call" | custom-call | tf_op jit(solution)/shard_map/middle/pallas_call | solution.py:283
  61.4 0.0 copy-start.9
  61.4 2.5 %collective-permute-start.8 = (bf16[2240,128]{1,0:T(8,128)(2,1)}, bf16[2240,128]{1,0:T(8,128)(2,1)S(1)}, u32[]{:S(2)}, u32[]{:S(2)}) collective-permute-start(bf16[2240,128]{1,0:T(8,128)(2,1)} %get-tuple-element.29.att0_ref), channel_id=1, source_target_pairs={{0,1},{1,2},{2,3},{3,4},{4,5},{5,6},{6,7},{7,8},{8,9},{9,10},{10,1... | collective-permute-start | bytes 1720328 | tf_op jit(solution)/shard_map/ppermute | solution.py:312
  63.9 6.4 %all-to-all-start.2 = ((bf16[16,144,128]{2,1,0:T(8,128)(2,1)}), bf16[16,144,128]{2,1,0:T(8,128)(2,1)S(1)}, u32[]{:S(2)}, u32[]{:S(2)}) async-start(bf16[16,144,128]{2,1,0:T(8,128)(2,1)} %bitcast.47), calls=%async_computation.2 | async-start | bytes 1179648 | tf_op jit(solution)/shard_map/all_to_all | solution.py:306
  70.3 0.0 copy-done.9
  70.3 0.1 collective-permute-start.4
  70.4 2.0 %collective-permute-start.3 = (f32[48,128]{1,0:T(8,128)S(1)}, f32[48,128]{1,0:T(8,128)S(1)}, u32[]{:S(2)}, u32[]{:S(2)}) collective-permute-start(f32[48,128]{1,0:T(8,128)S(1)} %copy-done.9), channel_id=1, source_target_pairs={{0,32},{16,48},{32,0},{48,16},{64,96},{80,112},{96,64},{112,80},{1... | collective-permute-start | bytes 73736 | tf_op jit(solution)/shard_map/ppermute | solution.py:320
  72.4 0.0 collective-permute-start.2
  72.4 1.2 %collective-permute-done.4 = f32[48,128]{1,0:T(8,128)S(1)} collective-permute-done((f32[48,128]{1,0:T(8,128)S(1)}, f32[48,128]{1,0:T(8,128)S(1)}, u32[]{:S(2)}, u32[]{:S(2)}) %collective-permute-start.4) | collective-permute-done | bytes 24608 | tf_op jit(solution)/shard_map/ppermute | solution.py:320
  73.7 0.7 collective-permute-done.3
  74.4 0.0 collective-permute-done.2
  74.4 6.5 %collective-permute-start.7 = (f32[48,128]{1,0:T(8,128)S(1)}, f32[48,128]{1,0:T(8,128)S(1)}, u32[]{:S(2)}, u32[]{:S(2)}) collective-permute-start(f32[48,128]{1,0:T(8,128)S(1)} %add_add_fusion.1), channel_id=1, source_target_pairs={{0,192},{16,208},{32,224},{48,240},{64,128},{80,144},{96,160},{112... | collective-permute-start | bytes 73736 | tf_op jit(solution)/shard_map/ppermute | solution.py:320
  80.9 1.0 collective-permute-start.6
  81.9 1.5 %collective-permute-start.5 = (f32[48,128]{1,0:T(8,128)S(1)}, f32[48,128]{1,0:T(8,128)S(1)}, u32[]{:S(2)}, u32[]{:S(2)}) collective-permute-start(f32[48,128]{1,0:T(8,128)S(1)} %add_add_fusion.1), channel_id=1, source_target_pairs={{0,64},{16,80},{32,96},{48,112},{64,0},{80,16},{96,32},{112,48},{1... | collective-permute-start | bytes 73736 | tf_op jit(solution)/shard_map/ppermute | solution.py:320
  83.4 0.0 collective-permute-done.7
  83.4 5.5 %collective-permute-done.6 = f32[48,128]{1,0:T(8,128)S(1)} collective-permute-done((f32[48,128]{1,0:T(8,128)S(1)}, f32[48,128]{1,0:T(8,128)S(1)}, u32[]{:S(2)}, u32[]{:S(2)}) %collective-permute-start.6) | collective-permute-done | bytes 24608 | tf_op jit(solution)/shard_map/ppermute | solution.py:320
  88.9 0.0 collective-permute-done.5
  88.9 0.6 add_add_fusion.conv_ref
  89.5 0.0 all-to-all-done.2.x_ref
  89.5 0.0 copy-start.4
  89.5 0.8 copy-done.4
  90.3 2.4 %scan_back.1 = bf16[16,192,128]{2,1,0:T(8,128)(2,1)} custom-call(bf16[16,144,128]{2,1,0:T(8,128)(2,1)} %copy-done.4, f32[48,128]{1,0:T(8,128)} %add_add_fusion.conv_ref), custom_call_target="tpu_custom_call" | custom-call | tf_op jit(solution)/shard_map/scan_back/pallas_call | solution.py:297
  92.8 0.0 collective-permute-done.9.ahead2_ref
  92.8 0.0 copy-start.6
  92.8 0.0 collective-permute-done.8.behind2_ref
  92.8 0.0 copy-start.7
  92.8 7.2 %all-to-all-start.3 = ((bf16[16,192,128]{2,1,0:T(8,128)(2,1)}), bf16[16,192,128]{2,1,0:T(8,128)(2,1)S(1)}, u32[]{:S(2)}, u32[]{:S(2)}) async-start(bf16[16,192,128]{2,1,0:T(8,128)(2,1)} %scan_back.1), calls=%async_computation.3 | async-start | bytes 1572864 | tf_op jit(solution)/shard_map/all_to_all | solution.py:306
  100.0 0.0 copy-done.7
  100.0 3.7 %mixed.1 = bf16[2240,256]{1,0:T(8,128)(2,1)} custom-call(bf16[2240,128]{1,0:T(8,128)(2,1)} %get-tuple-element.29.att0_ref, bf16[2240,128]{1,0:T(8,128)(2,1)} %get-tuple-element.30.att1_ref, bf16[2240,128]{1,0:T(8,128)(2,1)} %get-tuple-element.31.behind_ref, bf16[2240,128]{1,0:T(8,128)(2,1)} %copy-done.7, f32[2240,2]{1,0:T(8,128)} %bitcast.30), custom_call_target="tpu_custom_call" | custom-call | tf_op jit(solution)/shard_map/mixed/pallas_call | solution.py:283
  103.7 0.0 copy-done.6
  103.7 6.7 %queries.1 = bf16[2240,256]{1,0:T(8,128)(2,1)} custom-call(bf16[2240,256]{1,0:T(8,128)(2,1)} %bitcast.37, bf16[2240,256]{1,0:T(8,128)(2,1)} %bitcast.33, bf16[2240,128]{1,0:T(8,128)(2,1)} %copy-done.5, bf16[2240,128]{1,0:T(8,128)(2,1)} %copy-done.6, f32[2240,2]{1,0:T(8,128)} %bitcast.31, bf16[2304,128]{1,0:T(8,128)(2,1)} %bitcast.39, ...), custom_call_target="tpu_custom_call" | custom-call | tf_op jit(solution)/shard_map/queries/pallas_call | solution.py:283
  110.4 1.5 %all-to-all-done.3 = bf16[16,192,128]{2,1,0:T(8,128)(2,1)S(1)} async-done(((bf16[16,192,128]{2,1,0:T(8,128)(2,1)}), bf16[16,192,128]{2,1,0:T(8,128)(2,1)S(1)}, u32[]{:S(2)}, u32[]{:S(2)}) %all-to-all-start.3) | async-done | bytes 786464 | tf_op jit(solution)/shard_map/all_to_all | solution.py:306
  111.9 0.0 copy-start.2
  111.9 0.9 copy-done.2
  112.8 5.3 %last.1 = (bf16[2240,256]{1,0:T(8,128)(2,1)}, bf16[2240,256]{1,0:T(8,128)(2,1)}, f32[48,128]{1,0:T(8,128)}) custom-call(bf16[2240,256]{1,0:T(8,128)(2,1)} %bitcast.41, bf16[2240,256]{1,0:T(8,128)(2,1)} %bitcast.43, bf16[3072,128]{1,0:T(8,128)(2,1)} %bitcast.44, f32[2304,128]{1,0:T(8,128)} %get-tuple-element.40.gtot_ref, f32[2304,128]{1,0:T(8,128)} %get-tuple-element.41.glast_ref), custom_call_target="tpu_custom_call" | custom-call | tf_op jit(solution)/shard_map/last/pallas_call | solution.py:283
  118.1 0.7 slice.18
  118.8 0.7 div.10
  (3 shorter events, 0.0 us)
Async XLA Ops:
  2.5 50.0 %collective-permute-start = (bf16[2240,128]{1,0:T(8,128)(2,1)}, bf16[2240,128]{1,0:T(8,128)(2,1)S(1)}, u32[]{:S(2)}, u32[]{:S(2)}) collective-permute-start(bf16[2240,128]{1,0:T(8,128)(2,1)} %slice.20), channel_id=1, source_target_pairs={{0,1},{1,2},{2,3},{3,4},{4,5},{5,6},{6,7},{7,8},{8,9},{9,10},{10,1... | collective-permute-start | bytes 1720328 | tf_op jit(solution)/shard_map/ppermute | solution.py:312
  9.7 7.3 %copy-start = (bf16[1,256,2240]{1,2,0:T(8,128)(2,1)S(1)}, bf16[1,256,2240]{1,2,0:T(8,128)(2,1)}, u32[]{:S(2)}) copy-start(bf16[1,256,2240]{1,2,0:T(8,128)(2,1)} %param.8) | copy-start | bytes 3440644
  9.7 19.6 %all-to-all-start = ((bf16[16,144,128]{2,1,0:T(8,128)(2,1)}), bf16[16,144,128]{2,1,0:T(8,128)(2,1)S(1)}, u32[]{:S(2)}, u32[]{:S(2)}) async-start(bf16[16,144,128]{2,1,0:T(8,128)(2,1)} %bitcast.48), calls=%async_computation | async-start | bytes 1179648 | tf_op jit(solution)/shard_map/all_to_all | solution.py:306
  17.1 21.3 %copy-start.10 = (f32[2,2240]{1,0:T(2,128)S(1)}, f32[2,2240]{1,0:T(2,128)}, u32[]{:S(2)}) copy-start(f32[2,2240]{1,0:T(2,128)} %param.9) | copy-start | bytes 53764
  17.1 35.4 %collective-permute-start.1 = (bf16[2240,128]{1,0:T(8,128)(2,1)S(1)}, bf16[2240,128]{1,0:T(8,128)(2,1)S(1)}, u32[]{:S(2)}, u32[]{:S(2)}) collective-permute-start(bf16[2240,128]{1,0:T(8,128)(2,1)S(1)} %get-tuple-element.46), channel_id=1, source_target_pairs={{1,0},{2,1},{3,2},{4,3},{5,4},{6,5},{7,6},{8,7},{9,8},{10,9},{11,1... | collective-permute-start | bytes 1720328 | tf_op jit(solution)/shard_map/ppermute | solution.py:312
  29.3 0.8 copy-start.3
  33.2 15.9 %all-to-all-start.1 = ((bf16[16,144,128]{2,1,0:T(8,128)(2,1)}), bf16[16,144,128]{2,1,0:T(8,128)(2,1)S(1)}, u32[]{:S(2)}, u32[]{:S(2)}) async-start(bf16[16,144,128]{2,1,0:T(8,128)(2,1)} %scan.1), calls=%async_computation.1 | async-start | bytes 1179648 | tf_op jit(solution)/shard_map/all_to_all | solution.py:306
  49.1 3.4 %copy-start.1 = (bf16[16,144,128]{2,1,0:T(8,128)(2,1)}, bf16[16,144,128]{2,1,0:T(8,128)(2,1)S(1)}, u32[]{:S(2)}) copy-start(bf16[16,144,128]{2,1,0:T(8,128)(2,1)S(1)} %all-to-all-done.1) | copy-start | bytes 1769476
  49.1 43.6 %collective-permute-start.9 = (bf16[2240,128]{1,0:T(8,128)(2,1)S(1)}, bf16[2240,128]{1,0:T(8,128)(2,1)S(1)}, u32[]{:S(2)}, u32[]{:S(2)}) collective-permute-start(bf16[2240,128]{1,0:T(8,128)(2,1)S(1)} %get-tuple-element.35), channel_id=1, source_target_pairs={{1,0},{2,1},{3,2},{4,3},{5,4},{6,5},{7,6},{8,7},{9,8},{10,9},{11,1... | collective-permute-start | bytes 1720328 | tf_op jit(solution)/shard_map/ppermute | solution.py:312
  52.5 0.8 copy-start.8
  52.5 1.0 copy-start.5
  61.4 8.9 %copy-start.9 = (f32[48,128]{1,0:T(8,128)S(1)}, f32[48,128]{1,0:T(8,128)}, u32[]{:S(2)}) copy-start(f32[48,128]{1,0:T(8,128)} %get-tuple-element.33) | copy-start | bytes 73732
  61.4 31.3 %collective-permute-start.8 = (bf16[2240,128]{1,0:T(8,128)(2,1)}, bf16[2240,128]{1,0:T(8,128)(2,1)S(1)}, u32[]{:S(2)}, u32[]{:S(2)}) collective-permute-start(bf16[2240,128]{1,0:T(8,128)(2,1)} %get-tuple-element.29.att0_ref), channel_id=1, source_target_pairs={{0,1},{1,2},{2,3},{3,4},{4,5},{5,6},{6,7},{7,8},{8,9},{9,10},{10,1... | collective-permute-start | bytes 1720328 | tf_op jit(solution)/shard_map/ppermute | solution.py:312
  63.9 25.6 %all-to-all-start.2 = ((bf16[16,144,128]{2,1,0:T(8,128)(2,1)}), bf16[16,144,128]{2,1,0:T(8,128)(2,1)S(1)}, u32[]{:S(2)}, u32[]{:S(2)}) async-start(bf16[16,144,128]{2,1,0:T(8,128)(2,1)} %bitcast.47), calls=%async_computation.2 | async-start | bytes 1179648 | tf_op jit(solution)/shard_map/all_to_all | solution.py:306
  70.3 3.3 %collective-permute-start.4 = (f32[48,128]{1,0:T(8,128)S(1)}, f32[48,128]{1,0:T(8,128)S(1)}, u32[]{:S(2)}, u32[]{:S(2)}) collective-permute-start(f32[48,128]{1,0:T(8,128)S(1)} %copy-done.9), channel_id=1, source_target_pairs={{0,48},{16,32},{32,16},{48,0},{64,112},{80,96},{96,80},{112,64},{1... | collective-permute-start | bytes 73736 | tf_op jit(solution)/shard_map/ppermute | solution.py:320
  70.4 4.0 %collective-permute-start.3 = (f32[48,128]{1,0:T(8,128)S(1)}, f32[48,128]{1,0:T(8,128)S(1)}, u32[]{:S(2)}, u32[]{:S(2)}) collective-permute-start(f32[48,128]{1,0:T(8,128)S(1)} %copy-done.9), channel_id=1, source_target_pairs={{0,32},{16,48},{32,0},{48,16},{64,96},{80,112},{96,64},{112,80},{1... | collective-permute-start | bytes 73736 | tf_op jit(solution)/shard_map/ppermute | solution.py:320
  72.4 2.0 %collective-permute-start.2 = (f32[48,128]{1,0:T(8,128)S(1)}, f32[48,128]{1,0:T(8,128)S(1)}, u32[]{:S(2)}, u32[]{:S(2)}) collective-permute-start(f32[48,128]{1,0:T(8,128)S(1)} %copy-done.9), channel_id=1, source_target_pairs={{0,16},{16,0},{32,48},{48,32},{64,80},{80,64},{96,112},{112,96},{1... | collective-permute-start | bytes 73736 | tf_op jit(solution)/shard_map/ppermute | solution.py:320
  74.4 9.0 %collective-permute-start.7 = (f32[48,128]{1,0:T(8,128)S(1)}, f32[48,128]{1,0:T(8,128)S(1)}, u32[]{:S(2)}, u32[]{:S(2)}) collective-permute-start(f32[48,128]{1,0:T(8,128)S(1)} %add_add_fusion.1), channel_id=1, source_target_pairs={{0,192},{16,208},{32,224},{48,240},{64,128},{80,144},{96,160},{112... | collective-permute-start | bytes 73736 | tf_op jit(solution)/shard_map/ppermute | solution.py:320
  80.9 8.0 %collective-permute-start.6 = (f32[48,128]{1,0:T(8,128)S(1)}, f32[48,128]{1,0:T(8,128)S(1)}, u32[]{:S(2)}, u32[]{:S(2)}) collective-permute-start(f32[48,128]{1,0:T(8,128)S(1)} %add_add_fusion.1), channel_id=1, source_target_pairs={{0,128},{16,144},{32,160},{48,176},{64,192},{80,208},{96,224},{112... | collective-permute-start | bytes 73736 | tf_op jit(solution)/shard_map/ppermute | solution.py:320
  81.9 7.0 %collective-permute-start.5 = (f32[48,128]{1,0:T(8,128)S(1)}, f32[48,128]{1,0:T(8,128)S(1)}, u32[]{:S(2)}, u32[]{:S(2)}) collective-permute-start(f32[48,128]{1,0:T(8,128)S(1)} %add_add_fusion.1), channel_id=1, source_target_pairs={{0,64},{16,80},{32,96},{48,112},{64,0},{80,16},{96,32},{112,48},{1... | collective-permute-start | bytes 73736 | tf_op jit(solution)/shard_map/ppermute | solution.py:320
  89.5 0.8 copy-start.4
  92.8 11.0 %copy-start.6 = (bf16[2240,128]{1,0:T(8,128)(2,1)}, bf16[2240,128]{1,0:T(8,128)(2,1)S(1)}, u32[]{:S(2)}) copy-start(bf16[2240,128]{1,0:T(8,128)(2,1)S(1)} %collective-permute-done.9.ahead2_ref) | copy-start | bytes 1720324
  92.8 7.3 %copy-start.7 = (bf16[2240,128]{1,0:T(8,128)(2,1)}, bf16[2240,128]{1,0:T(8,128)(2,1)S(1)}, u32[]{:S(2)}) copy-start(bf16[2240,128]{1,0:T(8,128)(2,1)S(1)} %collective-permute-done.8.behind2_ref) | copy-start | bytes 1720324
  92.8 19.1 %all-to-all-start.3 = ((bf16[16,192,128]{2,1,0:T(8,128)(2,1)}), bf16[16,192,128]{2,1,0:T(8,128)(2,1)S(1)}, u32[]{:S(2)}, u32[]{:S(2)}) async-start(bf16[16,192,128]{2,1,0:T(8,128)(2,1)} %scan_back.1), calls=%async_computation.3 | async-start | bytes 1572864 | tf_op jit(solution)/shard_map/all_to_all | solution.py:306
  111.9 0.9 copy-start.2

commit v4 on v3

--- a/solution.py
+++ b/solution.py
@@ -312,14 +312,10 @@
     return lax.ppermute(block, axis, route)
 
 
-def total_over(x, axis):
+def total_over(x, axis, bit):
     n = lax.axis_size(axis)
-    bit = 1
-    while bit < n:
-        masks = [bit] if 2 * bit == n else [bit, 2 * bit, 3 * bit]
-        x = x + sum(lax.ppermute(x, axis, [(i, i ^ m) for i in range(n)]) for m in masks)
-        bit *= 4
-    return x
+    masks = [m for m in (bit, 2 * bit, 3 * bit) if m < n]
+    return x + sum(lax.ppermute(x, axis, [(i, i ^ m) for i in range(n)]) for m in masks)
 
 
 def body(queries, keys, values, cotangent, conv_weight):
@@ -347,7 +343,7 @@
         [half_tokens, half_tokens, half_tokens, state, state, sent, conv],
         q, behind, cot, ahead, weight, prev, tot, first, whole=[conv],
     )
-    conv = total_over(conv, "dp")
+    conv = total_over(conv, "dp", 1)
     got = exchange(send.reshape(n, chunk, LANES), "seq")
     att_behind2 = from_behind(att0, "seq", 1)
     follow = scan(scan_back_kernel, "scan_back", got, conv)
@@ -361,12 +357,14 @@
     (mixed,) = call(
         mixed_kernel, "mixed", [tokens], att0, att1, att_behind, att_behind2, weight
     )
+    follow, gq, mixed = lax.optimization_barrier((follow, gq, mixed))
     conv = shape(TOLD, LANES)
     gk, gv, conv = call(
         functools.partial(last_kernel, chunk), "last", [tokens, tokens, conv],
         k, v, follow, gtot, glast, whole=[conv],
     )
-    conv = conv[: 2 * HEADS].reshape(2, HEADS, LANES)[:, :, :HEAD_DIM].reshape(2, width)
+    conv = total_over(conv[: 2 * HEADS], "dp", 4)
+    conv = conv.reshape(2, HEADS, LANES)[:, :, :HEAD_DIM].reshape(2, width)
     conv = conv / (clips * lax.axis_size("dp"))
     return tuple(x.T.reshape(clips, toks, width) for x in (mixed, gq, gk, gv)) + (conv,)
 

time: 120 us -> 130 us (1.083)
  waiting for transfers between devices: 28.5 us -> 37.9 us
    all_to_all x4, waiting for transfers between devices: 21.1 us -> 30.6 us  [exchange(): return lax.all_to_all(x, axis, 0, 0, tiled=True)]
  transfers between devices with their start and end apart: 14 -> 14, of which waited for: 6 -> 7; matrix products, arithmetic and copies ran while one was open for 2% -> 2% of each run, Pallas kernels for 23% -> 21%
where the time goes in v4:
time: 130 us; the launch traced here: 129 us
  starting transfers between devices  47.8 us (37%)
  waiting for transfers between devices  37.9 us (29%)
  Pallas kernels  32.9 us (25%)
  local copies, waits for them, and re-layouts  8.35 us (6%)
  other arithmetic  1.36 us (1%)
    all_to_all x4, waiting for transfers between devices, exchange(): return lax.all_to_all(x, axis, 0, 0, tiled=True)  30.6 us
    pallas_call x5, Pallas kernels, call(): pl.pallas_call(kernel, grid=(2,), in_specs=[spec(a) for a in args], out_s...  27.3 us
    all_to_all x4, starting transfers between devices, exchange(): return lax.all_to_all(x, axis, 0, 0, tiled=True)  25.8 us
    ppermute x4, starting transfers between devices, from_behind(): return lax.ppermute(block, axis, route)  11.2 us
    ppermute x6, starting transfers between devices, total_over(): lax.ppermute(x, axis, [(i, i ^ m) for i in range(n)])  10.8 us
    ppermute x6, waiting for transfers between devices, total_over(): lax.ppermute(x, axis, [(i, i ^ m) for i in range(n)])  7.28 us
    pallas_call x2, Pallas kernels, scan(): pl.pallas_call(kernel, out_shape=shape(n, rows + sum((a.shape[0] for a in...  5.57 us
    unnamed x23, local copies, waits for them, and re-layouts  4.93 us
  transfers between devices with their start and end apart: 14, of which 7 were waited for; matrix products, arithmetic and copies ran while one was open for 2% of the time, Pallas kernels for 21%

profile of v4, /device:TPU:2, one launch (start us, length us, event | category | flops | bytes accessed | tf_op | source)
XLA Modules:
  0.0 129.0 jit_solution(15495892809505947546)
XLA Ops:
  0.6 1.9 %slice.20 = bf16[2240,128]{1,0:T(8,128)(2,1)} slice(bf16[2240,256]{1,0:T(8,128)(2,1)} %bitcast.35), slice={[0:2240], [128:256]} | slice | bytes 1146880 | tf_op jit(solution)/shard_map/slice | solution.py:333
  2.5 3.4 %collective-permute-start = (bf16[2240,128]{1,0:T(8,128)(2,1)}, bf16[2240,128]{1,0:T(8,128)(2,1)S(1)}, u32[]{:S(2)}, u32[]{:S(2)}) collective-permute-start(bf16[2240,128]{1,0:T(8,128)(2,1)} %slice.20), channel_id=1, source_target_pairs={{0,1},{1,2},{2,3},{3,4},{4,5},{5,6},{6,7},{7,8},{8,9},{9,10},{10,1... | collective-permute-start | bytes 1720328 | tf_op jit(solution)/shard_map/ppermute | solution.py:312
  5.9 3.7 %states.1 = (f32[2304,128]{1,0:T(8,128)}, f32[2304,128]{1,0:T(8,128)}, bf16[2304,128]{1,0:T(8,128)(2,1)}) custom-call(bf16[2240,256]{1,0:T(8,128)(2,1)} %bitcast.40, bf16[2240,256]{1,0:T(8,128)(2,1)} %bitcast.42), custom_call_target="tpu_custom_call" | custom-call | tf_op jit(solution)/shard_map/states/pallas_call | solution.py:283
  9.7 0.0 copy-start
  9.7 7.3 %all-to-all-start = ((bf16[16,144,128]{2,1,0:T(8,128)(2,1)}), bf16[16,144,128]{2,1,0:T(8,128)(2,1)S(1)}, u32[]{:S(2)}, u32[]{:S(2)}) async-start(bf16[16,144,128]{2,1,0:T(8,128)(2,1)} %bitcast.48), calls=%async_computation | async-start | bytes 1179648 | tf_op jit(solution)/shard_map/all_to_all | solution.py:306
  17.0 0.0 copy-done
  17.0 0.1 fusion
  17.1 0.0 copy-start.10
  17.1 2.0 %collective-permute-start.1 = (bf16[2240,128]{1,0:T(8,128)(2,1)S(1)}, bf16[2240,128]{1,0:T(8,128)(2,1)S(1)}, u32[]{:S(2)}, u32[]{:S(2)}) collective-permute-start(bf16[2240,128]{1,0:T(8,128)(2,1)S(1)} %get-tuple-element.52), channel_id=1, source_target_pairs={{1,0},{2,1},{3,2},{4,3},{5,4},{6,5},{7,6},{8,7},{9,8},{10,9},{11,1... | collective-permute-start | bytes 1720328 | tf_op jit(solution)/shard_map/ppermute | solution.py:312
  19.1 10.2 %all-to-all-done.x_ref = bf16[16,144,128]{2,1,0:T(8,128)(2,1)S(1)} async-done(((bf16[16,144,128]{2,1,0:T(8,128)(2,1)}), bf16[16,144,128]{2,1,0:T(8,128)(2,1)S(1)}, u32[]{:S(2)}, u32[]{:S(2)}) %all-to-all-start) | async-done | bytes 589856 | tf_op jit(solution)/shard_map/all_to_all | solution.py:306
  29.3 0.0 copy-start.3
  29.3 0.8 copy-done.3
  30.1 3.1 %scan.1 = bf16[16,144,128]{2,1,0:T(8,128)(2,1)} custom-call(bf16[16,144,128]{2,1,0:T(8,128)(2,1)} %copy-done.3), custom_call_target="tpu_custom_call" | custom-call | tf_op jit(solution)/shard_map/scan/pallas_call | solution.py:297
  33.2 5.1 %all-to-all-start.1 = ((bf16[16,144,128]{2,1,0:T(8,128)(2,1)}), bf16[16,144,128]{2,1,0:T(8,128)(2,1)S(1)}, u32[]{:S(2)}, u32[]{:S(2)}) async-start(bf16[16,144,128]{2,1,0:T(8,128)(2,1)} %scan.1), calls=%async_computation.1 | async-start | bytes 1179648 | tf_op jit(solution)/shard_map/all_to_all | solution.py:306
  38.4 0.0 copy-done.10
  38.4 1.4 %copy.11 = f32[2,2240]{0,1:T(8,128)} copy(f32[2,2240]{1,0:T(2,128)S(1)} %copy-done.10) | data formatting | bytes 35840 | tf_op args[4]
  39.8 9.4 %all-to-all-done.1 = bf16[16,144,128]{2,1,0:T(8,128)(2,1)S(1)} async-done(((bf16[16,144,128]{2,1,0:T(8,128)(2,1)}), bf16[16,144,128]{2,1,0:T(8,128)(2,1)S(1)}, u32[]{:S(2)}, u32[]{:S(2)}) %all-to-all-start.1) | async-done | bytes 589856 | tf_op jit(solution)/shard_map/all_to_all | solution.py:306
  49.1 0.0 copy-start.1
  49.1 3.4 %collective-permute-start.6 = (bf16[2240,128]{1,0:T(8,128)(2,1)S(1)}, bf16[2240,128]{1,0:T(8,128)(2,1)S(1)}, u32[]{:S(2)}, u32[]{:S(2)}) collective-permute-start(bf16[2240,128]{1,0:T(8,128)(2,1)S(1)} %get-tuple-element.36), channel_id=1, source_target_pairs={{1,0},{2,1},{3,2},{4,3},{5,4},{6,5},{7,6},{8,7},{9,8},{10,9},{11,1... | collective-permute-start | bytes 1720328 | tf_op jit(solution)/shard_map/ppermute | solution.py:312
  52.5 0.0 collective-permute-done.behind_ref
  52.5 0.0 copy-start.7
  52.5 0.0 collective-permute-done.1.ahead_ref
  52.5 0.0 copy-start.5
  52.5 0.0 copy-done.1
  52.5 0.8 copy-done.7
  53.3 0.2 copy-done.5
  53.5 7.9 %middle.1 = (bf16[2240,128]{1,0:T(8,128)(2,1)}, bf16[2240,128]{1,0:T(8,128)(2,1)}, bf16[2240,128]{1,0:T(8,128)(2,1)}, f32[2304,128]{1,0:T(8,128)}, f32[2304,128]...) custom-call(bf16[2240,256]{1,0:T(8,128)(2,1)} %bitcast.36, bf16[2240,128]{1,0:T(8,128)(2,1)} %copy-done.7, ...), custom_call_target="tpu_custom_call" | custom-call | tf_op jit(solution)/shard_map/middle/pallas_call | solution.py:283
  61.4 0.0 copy-start.9
  61.4 2.5 %collective-permute-start.5 = (bf16[2240,128]{1,0:T(8,128)(2,1)}, bf16[2240,128]{1,0:T(8,128)(2,1)S(1)}, u32[]{:S(2)}, u32[]{:S(2)}) collective-permute-start(bf16[2240,128]{1,0:T(8,128)(2,1)} %get-tuple-element.34.att0_ref), channel_id=1, source_target_pairs={{0,1},{1,2},{2,3},{3,4},{4,5},{5,6},{6,7},{7,8},{8,9},{9,10},{10,1... | collective-permute-start | bytes 1720328 | tf_op jit(solution)/shard_map/ppermute | solution.py:312
  63.9 6.4 %all-to-all-start.2 = ((bf16[16,144,128]{2,1,0:T(8,128)(2,1)}), bf16[16,144,128]{2,1,0:T(8,128)(2,1)S(1)}, u32[]{:S(2)}, u32[]{:S(2)}) async-start(bf16[16,144,128]{2,1,0:T(8,128)(2,1)} %bitcast.47), calls=%async_computation.2 | async-start | bytes 1179648 | tf_op jit(solution)/shard_map/all_to_all | solution.py:306
  70.3 0.0 copy-done.9
  70.3 0.1 collective-permute-start.4
  70.4 2.0 %collective-permute-start.3 = (f32[48,128]{1,0:T(8,128)S(1)}, f32[48,128]{1,0:T(8,128)S(1)}, u32[]{:S(2)}, u32[]{:S(2)}) collective-permute-start(f32[48,128]{1,0:T(8,128)S(1)} %copy-done.9), channel_id=1, source_target_pairs={{0,32},{16,48},{32,0},{48,16},{64,96},{80,112},{96,64},{112,80},{1... | collective-permute-start | bytes 73736 | tf_op jit(solution)/shard_map/ppermute | solution.py:318
  72.4 0.0 collective-permute-start.2
  72.4 1.2 collective-permute-done.4
  73.7 0.7 collective-permute-done.3
  74.4 0.0 collective-permute-done.2
  74.4 0.6 add_add_fusion.conv_ref
  75.0 7.9 %all-to-all-done.2.x_ref = bf16[16,144,128]{2,1,0:T(8,128)(2,1)S(1)} async-done(((bf16[16,144,128]{2,1,0:T(8,128)(2,1)}), bf16[16,144,128]{2,1,0:T(8,128)(2,1)S(1)}, u32[]{:S(2)}, u32[]{:S(2)}) %all-to-all-start.2) | async-done | bytes 589856 | tf_op jit(solution)/shard_map/all_to_all | solution.py:306
  82.9 0.0 copy-start.4
  82.9 0.8 copy-done.4
  83.7 2.4 %scan_back.1 = bf16[16,192,128]{2,1,0:T(8,128)(2,1)} custom-call(bf16[16,144,128]{2,1,0:T(8,128)(2,1)} %copy-done.4, f32[48,128]{1,0:T(8,128)} %add_add_fusion.conv_ref), custom_call_target="tpu_custom_call" | custom-call | tf_op jit(solution)/shard_map/scan_back/pallas_call | solution.py:297
  86.2 0.0 collective-permute-done.6.ahead2_ref
  86.2 0.0 copy-start.6
  86.2 0.0 collective-permute-done.5.behind2_ref
  86.2 0.0 copy-start.8
  86.2 7.0 %all-to-all-start.3 = ((bf16[16,192,128]{2,1,0:T(8,128)(2,1)}), bf16[16,192,128]{2,1,0:T(8,128)(2,1)S(1)}, u32[]{:S(2)}, u32[]{:S(2)}) async-start(bf16[16,192,128]{2,1,0:T(8,128)(2,1)} %scan_back.1), calls=%async_computation.3 | async-start | bytes 1572864 | tf_op jit(solution)/shard_map/all_to_all | solution.py:306
  93.2 0.0 copy-done.8
  93.2 3.7 %mixed.1 = bf16[2240,256]{1,0:T(8,128)(2,1)} custom-call(bf16[2240,128]{1,0:T(8,128)(2,1)} %get-tuple-element.34.att0_ref, bf16[2240,128]{1,0:T(8,128)(2,1)} %get-tuple-element.40.att1_ref, bf16[2240,128]{1,0:T(8,128)(2,1)} %get-tuple-element.41.behind_ref, bf16[2240,128]{1,0:T(8,128)(2,1)} %copy-done.8, f32[2240,2]{1,0:T(8,128)} %bitcast.30), custom_call_target="tpu_custom_call" | custom-call | tf_op jit(solution)/shard_map/mixed/pallas_call | solution.py:283
  96.9 0.0 copy-done.6
  96.9 6.7 %queries.1 = bf16[2240,256]{1,0:T(8,128)(2,1)} custom-call(bf16[2240,256]{1,0:T(8,128)(2,1)} %bitcast.37, bf16[2240,256]{1,0:T(8,128)(2,1)} %bitcast.33, bf16[2240,128]{1,0:T(8,128)(2,1)} %copy-done.5, bf16[2240,128]{1,0:T(8,128)(2,1)} %copy-done.6, f32[2240,2]{1,0:T(8,128)} %bitcast.31, bf16[2304,128]{1,0:T(8,128)(2,1)} %bitcast.39, ...), custom_call_target="tpu_custom_call" | custom-call | tf_op jit(solution)/shard_map/queries/pallas_call | solution.py:283
  103.5 3.1 %all-to-all-done.3 = bf16[16,192,128]{2,1,0:T(8,128)(2,1)S(1)} async-done(((bf16[16,192,128]{2,1,0:T(8,128)(2,1)}), bf16[16,192,128]{2,1,0:T(8,128)(2,1)S(1)}, u32[]{:S(2)}, u32[]{:S(2)}) %all-to-all-start.3) | async-done | bytes 786464 | tf_op jit(solution)/shard_map/all_to_all | solution.py:306
  106.6 0.0 copy-start.2
  106.6 0.9 copy-done.2
  107.5 5.3 %last.1 = (bf16[2240,256]{1,0:T(8,128)(2,1)}, bf16[2240,256]{1,0:T(8,128)(2,1)}, f32[48,128]{1,0:T(8,128)}) custom-call(bf16[2240,256]{1,0:T(8,128)(2,1)} %bitcast.41, bf16[2240,256]{1,0:T(8,128)(2,1)} %bitcast.43, bf16[3072,128]{1,0:T(8,128)(2,1)} %bitcast.44, f32[2304,128]{1,0:T(8,128)} %get-tuple-element.46.gtot_ref, f32[2304,128]{1,0:T(8,128)} %get-tuple-element.47.glast_ref), custom_call_target="tpu_custom_call" | custom-call | tf_op jit(solution)/shard_map/last/pallas_call | solution.py:283
  112.8 0.7 slice.18
  113.5 6.3 %collective-permute-start.9 = (f32[40,128]{1,0:T(8,128)S(1)}, f32[40,128]{1,0:T(8,128)S(1)}, u32[]{:S(2)}, u32[]{:S(2)}) collective-permute-start(f32[40,128]{1,0:T(8,128)S(1)} %slice.18), channel_id=1, source_target_pairs={{0,192},{16,208},{32,224},{48,240},{64,128},{80,144},{96,160},{112... | collective-permute-start | bytes 61448 | tf_op jit(solution)/shard_map/ppermute | solution.py:318
  119.9 0.9 collective-permute-start.8
  120.7 1.5 %collective-permute-start.7 = (f32[40,128]{1,0:T(8,128)S(1)}, f32[40,128]{1,0:T(8,128)S(1)}, u32[]{:S(2)}, u32[]{:S(2)}) collective-permute-start(f32[40,128]{1,0:T(8,128)S(1)} %slice.18), channel_id=1, source_target_pairs={{0,64},{16,80},{32,96},{48,112},{64,0},{80,16},{96,32},{112,48},{1... | collective-permute-start | bytes 61448 | tf_op jit(solution)/shard_map/ppermute | solution.py:318
  122.2 0.0 collective-permute-done.9
  122.2 5.3 %collective-permute-done.8 = f32[40,128]{1,0:T(8,128)S(1)} collective-permute-done((f32[40,128]{1,0:T(8,128)S(1)}, f32[40,128]{1,0:T(8,128)S(1)}, u32[]{:S(2)}, u32[]{:S(2)}) %collective-permute-start.8) | collective-permute-done | bytes 20512 | tf_op jit(solution)/shard_map/ppermute | solution.py:318
  127.5 0.0 collective-permute-done.7
  127.5 0.7 add_add_fusion.1
  128.3 0.7 div.10
  (2 shorter events, 0.0 us)
Async XLA Ops:
  2.5 50.0 %collective-permute-start = (bf16[2240,128]{1,0:T(8,128)(2,1)}, bf16[2240,128]{1,0:T(8,128)(2,1)S(1)}, u32[]{:S(2)}, u32[]{:S(2)}) collective-permute-start(bf16[2240,128]{1,0:T(8,128)(2,1)} %slice.20), channel_id=1, source_target_pairs={{0,1},{1,2},{2,3},{3,4},{4,5},{5,6},{6,7},{7,8},{8,9},{9,10},{10,1... | collective-permute-start | bytes 1720328 | tf_op jit(solution)/shard_map/ppermute | solution.py:312
  9.7 7.3 %copy-start = (bf16[1,256,2240]{1,2,0:T(8,128)(2,1)S(1)}, bf16[1,256,2240]{1,2,0:T(8,128)(2,1)}, u32[]{:S(2)}) copy-start(bf16[1,256,2240]{1,2,0:T(8,128)(2,1)} %param.8) | copy-start | bytes 3440644
  9.7 19.6 %all-to-all-start = ((bf16[16,144,128]{2,1,0:T(8,128)(2,1)}), bf16[16,144,128]{2,1,0:T(8,128)(2,1)S(1)}, u32[]{:S(2)}, u32[]{:S(2)}) async-start(bf16[16,144,128]{2,1,0:T(8,128)(2,1)} %bitcast.48), calls=%async_computation | async-start | bytes 1179648 | tf_op jit(solution)/shard_map/all_to_all | solution.py:306
  17.1 21.3 %copy-start.10 = (f32[2,2240]{1,0:T(2,128)S(1)}, f32[2,2240]{1,0:T(2,128)}, u32[]{:S(2)}) copy-start(f32[2,2240]{1,0:T(2,128)} %param.9) | copy-start | bytes 53764
  17.1 35.4 %collective-permute-start.1 = (bf16[2240,128]{1,0:T(8,128)(2,1)S(1)}, bf16[2240,128]{1,0:T(8,128)(2,1)S(1)}, u32[]{:S(2)}, u32[]{:S(2)}) collective-permute-start(bf16[2240,128]{1,0:T(8,128)(2,1)S(1)} %get-tuple-element.52), channel_id=1, source_target_pairs={{1,0},{2,1},{3,2},{4,3},{5,4},{6,5},{7,6},{8,7},{9,8},{10,9},{11,1... | collective-permute-start | bytes 1720328 | tf_op jit(solution)/shard_map/ppermute | solution.py:312
  29.3 0.8 copy-start.3
  33.2 15.9 %all-to-all-start.1 = ((bf16[16,144,128]{2,1,0:T(8,128)(2,1)}), bf16[16,144,128]{2,1,0:T(8,128)(2,1)S(1)}, u32[]{:S(2)}, u32[]{:S(2)}) async-start(bf16[16,144,128]{2,1,0:T(8,128)(2,1)} %scan.1), calls=%async_computation.1 | async-start | bytes 1179648 | tf_op jit(solution)/shard_map/all_to_all | solution.py:306
  49.1 3.4 %copy-start.1 = (bf16[16,144,128]{2,1,0:T(8,128)(2,1)}, bf16[16,144,128]{2,1,0:T(8,128)(2,1)S(1)}, u32[]{:S(2)}) copy-start(bf16[16,144,128]{2,1,0:T(8,128)(2,1)S(1)} %all-to-all-done.1) | copy-start | bytes 1769476
  49.1 37.0 %collective-permute-start.6 = (bf16[2240,128]{1,0:T(8,128)(2,1)S(1)}, bf16[2240,128]{1,0:T(8,128)(2,1)S(1)}, u32[]{:S(2)}, u32[]{:S(2)}) collective-permute-start(bf16[2240,128]{1,0:T(8,128)(2,1)S(1)} %get-tuple-element.36), channel_id=1, source_target_pairs={{1,0},{2,1},{3,2},{4,3},{5,4},{6,5},{7,6},{8,7},{9,8},{10,9},{11,1... | collective-permute-start | bytes 1720328 | tf_op jit(solution)/shard_map/ppermute | solution.py:312
  52.5 0.8 copy-start.7
  52.5 1.0 copy-start.5
  61.4 8.9 %copy-start.9 = (f32[48,128]{1,0:T(8,128)S(1)}, f32[48,128]{1,0:T(8,128)}, u32[]{:S(2)}) copy-start(f32[48,128]{1,0:T(8,128)} %get-tuple-element.33) | copy-start | bytes 73732
  61.4 24.7 %collective-permute-start.5 = (bf16[2240,128]{1,0:T(8,128)(2,1)}, bf16[2240,128]{1,0:T(8,128)(2,1)S(1)}, u32[]{:S(2)}, u32[]{:S(2)}) collective-permute-start(bf16[2240,128]{1,0:T(8,128)(2,1)} %get-tuple-element.34.att0_ref), channel_id=1, source_target_pairs={{0,1},{1,2},{2,3},{3,4},{4,5},{5,6},{6,7},{7,8},{8,9},{9,10},{10,1... | collective-permute-start | bytes 1720328 | tf_op jit(solution)/shard_map/ppermute | solution.py:312
  63.9 19.0 %all-to-all-start.2 = ((bf16[16,144,128]{2,1,0:T(8,128)(2,1)}), bf16[16,144,128]{2,1,0:T(8,128)(2,1)S(1)}, u32[]{:S(2)}, u32[]{:S(2)}) async-start(bf16[16,144,128]{2,1,0:T(8,128)(2,1)} %bitcast.47), calls=%async_computation.2 | async-start | bytes 1179648 | tf_op jit(solution)/shard_map/all_to_all | solution.py:306
  70.3 3.3 %collective-permute-start.4 = (f32[48,128]{1,0:T(8,128)S(1)}, f32[48,128]{1,0:T(8,128)S(1)}, u32[]{:S(2)}, u32[]{:S(2)}) collective-permute-start(f32[48,128]{1,0:T(8,128)S(1)} %copy-done.9), channel_id=1, source_target_pairs={{0,48},{16,32},{32,16},{48,0},{64,112},{80,96},{96,80},{112,64},{1... | collective-permute-start | bytes 73736 | tf_op jit(solution)/shard_map/ppermute | solution.py:318
  70.4 4.0 %collective-permute-start.3 = (f32[48,128]{1,0:T(8,128)S(1)}, f32[48,128]{1,0:T(8,128)S(1)}, u32[]{:S(2)}, u32[]{:S(2)}) collective-permute-start(f32[48,128]{1,0:T(8,128)S(1)} %copy-done.9), channel_id=1, source_target_pairs={{0,32},{16,48},{32,0},{48,16},{64,96},{80,112},{96,64},{112,80},{1... | collective-permute-start | bytes 73736 | tf_op jit(solution)/shard_map/ppermute | solution.py:318
  72.4 2.0 %collective-permute-start.2 = (f32[48,128]{1,0:T(8,128)S(1)}, f32[48,128]{1,0:T(8,128)S(1)}, u32[]{:S(2)}, u32[]{:S(2)}) collective-permute-start(f32[48,128]{1,0:T(8,128)S(1)} %copy-done.9), channel_id=1, source_target_pairs={{0,16},{16,0},{32,48},{48,32},{64,80},{80,64},{96,112},{112,96},{1... | collective-permute-start | bytes 73736 | tf_op jit(solution)/shard_map/ppermute | solution.py:318
  82.9 0.8 copy-start.4
  86.2 10.7 %copy-start.6 = (bf16[2240,128]{1,0:T(8,128)(2,1)}, bf16[2240,128]{1,0:T(8,128)(2,1)S(1)}, u32[]{:S(2)}) copy-start(bf16[2240,128]{1,0:T(8,128)(2,1)S(1)} %collective-permute-done.6.ahead2_ref) | copy-start | bytes 1720324
  86.2 7.0 %copy-start.8 = (bf16[2240,128]{1,0:T(8,128)(2,1)}, bf16[2240,128]{1,0:T(8,128)(2,1)S(1)}, u32[]{:S(2)}) copy-start(bf16[2240,128]{1,0:T(8,128)(2,1)S(1)} %collective-permute-done.5.behind2_ref) | copy-start | bytes 1720324
  86.2 20.4 %all-to-all-start.3 = ((bf16[16,192,128]{2,1,0:T(8,128)(2,1)}), bf16[16,192,128]{2,1,0:T(8,128)(2,1)S(1)}, u32[]{:S(2)}, u32[]{:S(2)}) async-start(bf16[16,192,128]{2,1,0:T(8,128)(2,1)} %scan_back.1), calls=%async_computation.3 | async-start | bytes 1572864 | tf_op jit(solution)/shard_map/all_to_all | solution.py:306
  106.6 0.9 copy-start.2
  113.5 8.7 %collective-permute-start.9 = (f32[40,128]{1,0:T(8,128)S(1)}, f32[40,128]{1,0:T(8,128)S(1)}, u32[]{:S(2)}, u32[]{:S(2)}) collective-permute-start(f32[40,128]{1,0:T(8,128)S(1)} %slice.18), channel_id=1, source_target_pairs={{0,192},{16,208},{32,224},{48,240},{64,128},{80,144},{96,160},{112... | collective-permute-start | bytes 61448 | tf_op jit(solution)/shard_map/ppermute | solution.py:318
  119.9 7.7 %collective-permute-start.8 = (f32[40,128]{1,0:T(8,128)S(1)}, f32[40,128]{1,0:T(8,128)S(1)}, u32[]{:S(2)}, u32[]{:S(2)}) collective-permute-start(f32[40,128]{1,0:T(8,128)S(1)} %slice.18), channel_id=1, source_target_pairs={{0,128},{16,144},{32,160},{48,176},{64,192},{80,208},{96,224},{112... | collective-permute-start | bytes 61448 | tf_op jit(solution)/shard_map/ppermute | solution.py:318
  120.7 6.8 %collective-permute-start.7 = (f32[40,128]{1,0:T(8,128)S(1)}, f32[40,128]{1,0:T(8,128)S(1)}, u32[]{:S(2)}, u32[]{:S(2)}) collective-permute-start(f32[40,128]{1,0:T(8,128)S(1)} %slice.18), channel_id=1, source_target_pairs={{0,64},{16,80},{32,96},{48,112},{64,0},{80,16},{96,32},{112,48},{1... | collective-permute-start | bytes 61448 | tf_op jit(solution)/shard_map/ppermute | solution.py:318
